TPU v7x, 256 devices: a whole 4x4x8 slice. The times are simulated.
256 devices in a mesh: gx: 8 (over z), gy: 4 (over x_lo, core), gz: 8 (over y, x_hi).
Axes of the slice: x: 4 (x_hi: 2, x_lo: 2; x = x_hi * 2 + x_lo), y: 4, z: 8, core: 2. Of those that a mesh axis runs over, the one named last changes fastest.
Arguments:
- volume: float32 [256, 256, 256], P('gx', ('gy', 'gz')), may hold values from -12 to 12
- prior_weight: float32 [256, 256, 256], P('gx', ('gy', 'gz')), may hold values from 0.1 to 2
- kernel: float32 [512, 512, 512], P(('gy', 'gz'), 'gx'), may hold values from 0.05 to 1
Outputs:
- hessian_product: float32 [256, 256, 256], P('gx', ('gy', 'gz'))
- curvature: float32 [1], replicated
All inputs are finite; a program needn't handle non-finite values.
Results may differ from a plain program's by a relative error of at most 0.00005.
Values sent between devices are 32-bit elements; how exact they have to be, the bound alone decides.
No kernel may reach another device: no remote copies, remote signals or barrier semaphores. Data moves between devices by JAX's collectives and lax.ppermute only.
A program may use at most 64 MiB of HBM per device.

v0:
```python
import math

import jax
import jax.numpy as jnp
import ml_dtypes
import numpy as np
from jax import lax
from jax.experimental import pallas as pl
from jax.experimental.pallas import tpu as pltpu
from jax.sharding import PartitionSpec as P

M = 256
N = 512
GX = 8
GA = 32
BF = jnp.bfloat16
VMEM_LIMIT = 50 * 1024 * 1024


def trig(rows, cols):
    product = np.outer(np.asarray(rows), np.asarray(cols)) % N
    angle = product * (2.0 * math.pi / N)
    return np.cos(angle), np.sin(angle)


def halves(table):
    table = np.asarray(table, np.float32)
    high = table.astype(ml_dtypes.bfloat16)
    low = (table - high.astype(np.float32)).astype(ml_dtypes.bfloat16)
    return high, low


def z_forward_table():
    cosine, sine = trig(np.arange(M), np.arange(N))
    stacked = np.stack([cosine.reshape(M, GX, 64), -sine.reshape(M, GX, 64)], axis=2)
    return halves(stacked.reshape(M, GX * 128))


def x_forward_table():
    cosine, sine = trig(np.arange(N), np.arange(M))
    return halves(np.concatenate([cosine, sine], axis=1))


def y_inverse_table():
    cosine, sine = trig(np.arange(M), np.arange(N))
    return halves(np.concatenate([cosine, sine], axis=1))


def x_inverse_table():
    order = np.arange(N).reshape(GA, 16).T.reshape(-1)
    cosine, sine = trig(np.arange(M), order)
    return halves(np.concatenate([cosine, sine], axis=1))


def z_inverse_table():
    cosine, sine = trig(np.arange(N), np.arange(M))
    stacked = np.stack([cosine.reshape(GX, 64, M), -sine.reshape(GX, 64, M)], axis=1)
    return halves(stacked.reshape(GX * 128, M) / float(N) ** 3)


def split(value):
    high = value.astype(BF)
    low = (value - high.astype(jnp.float32)).astype(BF)
    return high, low


def dot(left, right):
    return jnp.dot(left, right, preferred_element_type=jnp.float32)


def dot3(left_high, left_low, right_high, right_low):
    return dot(left_high, right_high) + (dot(left_high, right_low) + dot(left_low, right_high))


def rotated(value, sign):
    lane = lax.broadcasted_iota(jnp.int32, value.shape, 1)
    swapped = pltpu.roll(value, 64, 1)
    return jnp.where(lane < 64, sign * swapped, -sign * swapped)


def fold(value):
    rows, cols = value.shape
    total = jnp.sum(value.reshape(rows // 8, 8, cols), axis=0)
    parts = [total[:, at : at + 128] for at in range(0, cols, 128)]
    return sum(parts[1:], parts[0])


def z_forward_kernel(volume, prior, high, low, out, partial):
    field = volume[...]
    partial[...] = fold((prior[...] * field * field).reshape(M, M))
    rows = jnp.concatenate([volume[:, y, :] for y in range(8)], axis=0)
    rows_high, rows_low = split(rows)
    for half in range(2):
        cols = slice(half * 512, half * 512 + 512)
        res = dot3(rows_high, rows_low, high[:, cols], low[:, cols])
        for block in range(4):
            out[half * 4 + block] = res[:, block * 128 : block * 128 + 128]


def x_forward_kernel(received, high, low, out):
    real = [received[:, y].reshape(M, 128) for y in range(2)]
    turned = [rotated(part, 1.0) for part in real]
    data = jnp.concatenate(
        [jnp.concatenate(real, axis=1), jnp.concatenate(turned, axis=1)], axis=0
    )
    data_high, data_low = split(data)
    res = dot3(high[...], low[...], data_high, data_low)
    for y in range(2):
        out[:, y] = res[:, y * 128 : y * 128 + 128].reshape(GA, 16, 128)


def y_kernel(received, weights, partial, fwd_high, fwd_low, inv_high, inv_low, out, total):
    step = pl.program_id(0)

    @pl.when(step == 0)
    def _():
        total[...] = jnp.zeros_like(total)

    real = [received[pl.ds(step * 2 + k, M, stride=16), :] for k in range(2)]
    turned = [rotated(part, 1.0) for part in real]
    data = jnp.concatenate(
        [jnp.concatenate(real, axis=1), jnp.concatenate(turned, axis=1)], axis=0
    )
    data_high, data_low = split(data)
    spectrum = dot3(fwd_high[...], fwd_low[...], data_high, data_low)
    scale = []
    for k in range(2):
        flipped = weights[k].T
        scale += [flipped, flipped]
    weighted = spectrum * jnp.concatenate(scale, axis=1)
    total[...] += fold(weighted * spectrum)
    back = jnp.concatenate(
        [rotated(weighted[:, :128], -1.0), rotated(weighted[:, 128:], -1.0)], axis=1
    )
    back_high, back_low = split(jnp.concatenate([weighted, back], axis=0))
    res = dot3(inv_high[...], inv_low[...], back_high, back_low)
    out[:, :, pl.ds(pl.multiple_of(step * 256, 256), 256)] = res.reshape(GA, 8, 256)

    @pl.when(step == 7)
    def _():
        count = total[...] * (1.0 / float(N) ** 3) + partial[...]
        out[:, :, 2048:] = jnp.broadcast_to(count[None], (GA, 8, 128))


def x_inverse_kernel(received, high, low, out):
    for pair in range(4):
        real = []
        for y in (2 * pair, 2 * pair + 1):
            real.append(
                jnp.concatenate(
                    [received[:, y, k * 128 : k * 128 + 128] for k in range(16)],
                    axis=0,
                )
            )
        turned = [rotated(part, -1.0) for part in real]
        data = jnp.concatenate(
            [jnp.concatenate(real, axis=1), jnp.concatenate(turned, axis=1)], axis=0
        )
        data_high, data_low = split(data)
        res = dot3(high[...], low[...], data_high, data_low)
        for at in range(2):
            y = 2 * pair + at
            out[:, y * 32 : y * 32 + 32, :] = res[:, at * 128 : at * 128 + 128].reshape(GX, 32, 128)
    group = jnp.sum(received[:, :, 2048:], axis=0)
    out[:, 256:, :] = jnp.broadcast_to(group[None], (GX, 8, 128))


def z_inverse_kernel(received, volume, prior, high, low, out, curvature):
    data = jnp.concatenate([received[c, :256, :] for c in range(GX)], axis=1)
    data_high, data_low = split(data)
    image = dot3(data_high, data_low, high[...], low[...])
    for y in range(8):
        out[:, y, :] = image[y * 32 : y * 32 + 32, :] + prior[:, y, :] * volume[:, y, :]
    total = jnp.sum(received[:, 256:, :], axis=0)
    curvature[...] = jnp.broadcast_to(jnp.sum(total) / float(M) ** 3, (8, 128))


def whole():
    return pl.BlockSpec(memory_space=pltpu.VMEM)


def params():
    return pltpu.CompilerParams(vmem_limit_bytes=VMEM_LIMIT)


def f32(*shape):
    return jax.ShapeDtypeStruct(shape, jnp.float32)


def local(volume, prior_weight, kernel):
    sent, partial = pl.pallas_call(
        z_forward_kernel,
        out_shape=(f32(GX, 256, 128), f32(8, 128)),
        in_specs=[whole()] * 4,
        out_specs=(whole(), whole()),
        compiler_params=params(),
        name="z_forward",
    )(volume, prior_weight, *z_forward_table())
    got = lax.all_to_all(sent, "gx", split_axis=0, concat_axis=0, tiled=True)
    sent = pl.pallas_call(
        x_forward_kernel,
        grid=(4,),
        out_shape=f32(GA, 8, 16, 128),
        in_specs=[pl.BlockSpec((GX, 2, 32, 128), lambda i: (0, i, 0, 0)), whole(), whole()],
        out_specs=pl.BlockSpec((GA, 2, 16, 128), lambda i: (0, i, 0, 0)),
        compiler_params=params(),
        name="x_forward",
    )(got.reshape(GX, 8, 32, 128), *x_forward_table())
    got = lax.all_to_all(sent, ("gy", "gz"), split_axis=0, concat_axis=0, tiled=True)
    sent = pl.pallas_call(
        y_kernel,
        grid=(8,),
        out_shape=f32(GA, 8, 2176),
        in_specs=[whole(), pl.BlockSpec((2, 64, 512), lambda i: (i, 0, 0))] + [whole()] * 5,
        out_specs=whole(),
        scratch_shapes=[pltpu.VMEM((8, 128), jnp.float32)],
        compiler_params=params(),
        name="y_both",
    )(got.reshape(GA * 8 * 16, 128), kernel, partial, *x_forward_table(), *y_inverse_table())
    got = lax.all_to_all(sent, ("gy", "gz"), split_axis=0, concat_axis=0, tiled=True)
    sent = pl.pallas_call(
        x_inverse_kernel,
        out_shape=f32(GX, 264, 128),
        in_specs=[whole()] * 3,
        out_specs=whole(),
        compiler_params=params(),
        name="x_inverse",
    )(got, *x_inverse_table())
    got = lax.all_to_all(sent, "gx", split_axis=0, concat_axis=0, tiled=True)
    product, curvature = pl.pallas_call(
        z_inverse_kernel,
        out_shape=(f32(32, 8, M), f32(8, 128)),
        in_specs=[whole()] * 5,
        out_specs=(whole(), whole()),
        compiler_params=params(),
        name="z_inverse",
    )(got, volume, prior_weight, *z_inverse_table())
    return product, curvature[0, :1]


def solution(mesh):
    return jax.shard_map(
        local,
        mesh=mesh,
        in_specs=(
            P("gx", ("gy", "gz"), None),
            P("gx", ("gy", "gz"), None),
            P(("gy", "gz"), "gx", None),
        ),
        out_specs=(P("gx", ("gy", "gz"), None), P()),
        check_vma=False,
    )
```

profile of v0, /device:TPU:1, one launch (start us, length us, event | category | flops | bytes accessed | tf_op | source)
XLA Modules:
  0.0 176.1 jit_solution(4179782759649545726)
XLA Ops:
  0.6 0.0 copy-start
  0.6 0.0 copy-start.1
  0.7 0.0 copy-start.2
  0.7 1.0 copy-done.2
  1.7 0.0 copy-start.4
  1.7 0.9 copy-done.4
  2.6 1.0 copy-done.8
  3.7 1.0 copy-done.9
  4.7 0.7 z_forward.1
  5.4 36.0 %all_to_all.20 = f32[8,256,128]{2,1,0:T(8,128)S(1)} all-to-all(f32[8,256,128]{2,1,0:T(8,128)S(1)} %get-tuple-element.6), channel_id=1, replica_groups=mesh['gx'=8,'gy'=4,'gz'=8] {'gx'}, dimensions={0} | all-to-all | bytes 2097152 | tf_op jit(solution)/shard_map/all_to_all | solution.py:199
  41.4 0.0 copy-done
  41.4 0.0 copy-done.1
  41.4 3.7 %x_forward.1 = f32[32,8,16,128]{3,2,1,0:T(8,128)} custom-call(f32[8,8,32,128]{3,2,1,0:T(8,128)S(1)} %bitcast.3, bf16[512,512]{1,0:T(8,128)(2,1)S(1)} %copy-done.1, bf16[512,512]{1,0:T(8,128)(2,1)S(1)} %copy-done), custom_call_target="tpu_custom_call" | custom-call | tf_op jit(solution)/shard_map/x_forward/pallas_call | solution.py:200
  45.2 38.2 %all_to_all.21 = f32[32,8,16,128]{3,2,1,0:T(8,128)} all-to-all(f32[32,8,16,128]{3,2,1,0:T(8,128)} %x_forward.1), channel_id=1, replica_groups=mesh['gx'=8,'gy'=4,'gz'=8] {'gy','gz'}, dimensions={0} | all-to-all | bytes 4194304 | tf_op jit(solution)/shard_map/all_to_all | solution.py:209
  83.4 0.0 copy-done.12
  83.4 0.0 copy-done.13
  83.4 18.3 %y_both.1 = f32[32,8,2176]{2,1,0:T(8,128)} custom-call(f32[4096,128]{1,0:T(8,128)} %bitcast.4, f32[16,64,512]{2,1,0:T(8,128)} %weights.1, f32[8,128]{1,0:T(8,128)S(1)} %get-tuple-element.7.partial, bf16[512,512]{1,0:T(8,128)(2,1)S(1)} %copy-done.1, bf16[512,512]{1,0:T(8,128)(2,1)S(1)} %copy-done, bf16[256,1024]{1,0:T(8,128)(2,1)S(1)} %copy-done.13, ...), custom_call_target="tpu_custom_call" | custom-call | tf_op jit(solution)/shard_map/y_both/pallas_call | solution.py:210
  101.7 36.3 %all_to_all.22.received = f32[32,8,2176]{2,1,0:T(8,128)} all-to-all(f32[32,8,2176]{2,1,0:T(8,128)} %y_both.1), channel_id=1, replica_groups=mesh['gx'=8,'gy'=4,'gz'=8] {'gy','gz'}, dimensions={0} | all-to-all | bytes 4456448 | tf_op jit(solution)/shard_map/all_to_all | solution.py:220
  137.9 0.0 copy-done.6
  137.9 0.0 copy-done.7
  137.9 4.1 %x_inverse.1 = f32[8,264,128]{2,1,0:T(8,128)S(1)} custom-call(f32[32,8,2176]{2,1,0:T(8,128)} %all_to_all.22.received, bf16[256,1024]{1,0:T(8,128)(2,1)S(1)} %copy-done.7, bf16[256,1024]{1,0:T(8,128)(2,1)S(1)} %copy-done.6), custom_call_target="tpu_custom_call" | custom-call | tf_op jit(solution)/shard_map/x_inverse/pallas_call | solution.py:221
  142.1 0.0 copy-start.3
  142.1 0.0 copy-start.5
  142.1 0.0 copy-start.10
  142.1 0.0 copy-start.11
  142.1 32.0 %all_to_all.23.received = f32[8,264,128]{2,1,0:T(8,128)S(1)} all-to-all(f32[8,264,128]{2,1,0:T(8,128)S(1)} %x_inverse.1), channel_id=1, replica_groups=mesh['gx'=8,'gy'=4,'gz'=8] {'gx'}, dimensions={0} | all-to-all | bytes 2162688 | tf_op jit(solution)/shard_map/all_to_all | solution.py:229
  174.2 0.0 copy-done.3
  174.2 0.0 copy-done.5
  174.2 0.0 copy-done.10
  174.2 0.0 copy-done.11
  174.2 1.4 z_inverse.1
  175.6 0.5 slice.3
  (6 shorter events, 0.0 us)
Async XLA Ops:
  0.6 40.8 %copy-start = (bf16[512,512]{1,0:T(8,128)(2,1)S(1)}, bf16[512,512]{1,0:T(8,128)(2,1)}, u32[]{:S(2)}) copy-start(bf16[512,512]{1,0:T(8,128)(2,1)} %constant.23.clone.low.fwd_low) | copy-start | bytes 1572868
  0.6 40.8 %copy-start.1 = (bf16[512,512]{1,0:T(8,128)(2,1)S(1)}, bf16[512,512]{1,0:T(8,128)(2,1)}, u32[]{:S(2)}) copy-start(bf16[512,512]{1,0:T(8,128)(2,1)} %constant.22.clone.high.fwd_high) | copy-start | bytes 1572868
  0.7 1.0 copy-start.2
  1.7 0.9 copy-start.4
  2.6 1.0 copy-start.8
  3.7 1.0 copy-start.9
  45.1 38.3 %copy-start.12 = (bf16[256,1024]{1,0:T(8,128)(2,1)S(1)}, bf16[256,1024]{1,0:T(8,128)(2,1)}, u32[]{:S(2)}) copy-start(bf16[256,1024]{1,0:T(8,128)(2,1)} %constant.25.clone.inv_low) | copy-start | bytes 1572868
  45.2 38.3 %copy-start.13 = (bf16[256,1024]{1,0:T(8,128)(2,1)S(1)}, bf16[256,1024]{1,0:T(8,128)(2,1)}, u32[]{:S(2)}) copy-start(bf16[256,1024]{1,0:T(8,128)(2,1)} %constant.24.clone.inv_high) | copy-start | bytes 1572868
  101.7 36.3 %copy-start.6 = (bf16[256,1024]{1,0:T(8,128)(2,1)S(1)}, bf16[256,1024]{1,0:T(8,128)(2,1)}, u32[]{:S(2)}) copy-start(bf16[256,1024]{1,0:T(8,128)(2,1)} %constant.27.clone.low) | copy-start | bytes 1572868
  101.7 36.3 %copy-start.7 = (bf16[256,1024]{1,0:T(8,128)(2,1)S(1)}, bf16[256,1024]{1,0:T(8,128)(2,1)}, u32[]{:S(2)}) copy-start(bf16[256,1024]{1,0:T(8,128)(2,1)} %constant.26.clone.high) | copy-start | bytes 1572868
  142.1 32.1 %copy-start.3 = (f32[32,8,256]{2,1,0:T(8,128)S(1)}, f32[32,8,256]{2,1,0:T(8,128)}, u32[]{:S(2)}) copy-start(f32[32,8,256]{2,1,0:T(8,128)} %volume.3) | copy-start | bytes 786436
  142.1 32.1 %copy-start.5 = (f32[32,8,256]{2,1,0:T(8,128)S(1)}, f32[32,8,256]{2,1,0:T(8,128)}, u32[]{:S(2)}) copy-start(f32[32,8,256]{2,1,0:T(8,128)} %prior.3) | copy-start | bytes 786436
  142.1 32.1 %copy-start.10 = (bf16[1024,256]{1,0:T(8,128)(2,1)S(1)}, bf16[1024,256]{1,0:T(8,128)(2,1)}, u32[]{:S(2)}) copy-start(bf16[1024,256]{1,0:T(8,128)(2,1)} %constant.29.clone.low) | copy-start | bytes 1572868
  142.1 32.1 %copy-start.11 = (bf16[1024,256]{1,0:T(8,128)(2,1)S(1)}, bf16[1024,256]{1,0:T(8,128)(2,1)}, u32[]{:S(2)}) copy-start(bf16[1024,256]{1,0:T(8,128)(2,1)} %constant.28.clone.high) | copy-start | bytes 1572868
where the time goes:
time: 177 us; the launch traced here: 176 us
  blocking collectives  143 us (81%)
  Pallas kernels  28.2 us (16%)
  local copies, waits for them, and re-layouts  4.63 us (3%)
    all_to_all x2, blocking collectives, local(): lax.all_to_all(sent, ('gy', 'gz'), split_axis=0, concat_axis=0, tiled=True)  74.5 us
    all_to_all x2, blocking collectives, local(): got = lax.all_to_all(sent, 'gx', split_axis=0, concat_axis=0, tiled=True)  68.1 us
    pallas_call x1, Pallas kernels, local(): pl.pallas_call(y_kernel, grid=(8,), out_shape=f32(GA, 8, 2176), in_specs=...  18.3 us
    pallas_call x1, Pallas kernels, local(): pl.pallas_call(x_inverse_kernel, out_shape=f32(GX, 264, 128), in_specs=[w...  4.13 us
    unnamed x28, local copies, waits for them, and re-layouts  4.12 us
    pallas_call x1, Pallas kernels, local(): pl.pallas_call(x_forward_kernel, grid=(4,), out_shape=f32(GA, 8, 16, 128)...  3.71 us

commit v1 on v0

v1 whole, which is shorter than its diff:
```python
import math

import jax
import jax.numpy as jnp
import ml_dtypes
import numpy as np
from jax import lax
from jax.experimental import pallas as pl
from jax.experimental.pallas import tpu as pltpu
from jax.sharding import PartitionSpec as P

M = 256
N = 512
GX = 8
GA = 32
HALF = 32
EARLY = 4
PACK_COST = 2
OWN_COST = 8
NEAR_COST = 20
FORWARD_COST = 5
AXES = ("gx", "gy", "gz")
BF = jnp.bfloat16
VMEM_LIMIT = 50 * 1024 * 1024


def trig(rows, cols):
    product = np.outer(np.asarray(rows), np.asarray(cols)) % N
    angle = product * (2.0 * math.pi / N)
    return np.cos(angle), np.sin(angle)


def halves(table):
    table = np.asarray(table, np.float32)
    high = table.astype(ml_dtypes.bfloat16)
    low = (table - high.astype(np.float32)).astype(ml_dtypes.bfloat16)
    return high, low


def z_forward_table():
    cosine, sine = trig(np.arange(M), np.arange(N))
    stacked = np.stack([cosine, -sine], axis=0).reshape(2, M, GX // 2, 2, 64)
    main = stacked[..., :HALF].transpose(1, 2, 0, 3, 4).reshape(M, GX * 64)
    edge = stacked[..., HALF].transpose(1, 2, 3, 0).reshape(M, GX * 2)
    return halves(np.concatenate([main, np.repeat(edge, 8, axis=1)], axis=1))


def z_inverse_table():
    cosine, sine = trig(np.arange(N), np.arange(M))
    stacked = np.stack([cosine, -sine], axis=0).reshape(2, GX // 2, 2, 64, M)
    main = stacked[:, :, :, :HALF].transpose(1, 0, 2, 3, 4).reshape(GX * 64, M)
    edge = stacked[:, :, :, HALF].transpose(1, 2, 0, 3).reshape(GX * 2, M)
    return halves(np.concatenate([main, np.repeat(edge, 8, axis=0)], axis=0) / float(N) ** 3)


def forward_table():
    cosine, sine = trig(np.arange(N), np.arange(M))
    return halves(np.concatenate([cosine, sine], axis=1))


def inverse_table():
    cosine, sine = trig(np.arange(M), np.arange(N))
    return halves(np.concatenate([cosine, sine], axis=1))


def x_inverse_table():
    order = np.arange(N).reshape(GA, 16).T.reshape(-1)
    cosine, sine = trig(np.arange(M), order)
    return halves(np.concatenate([cosine, sine], axis=1))


def flip_tables():
    flip = np.zeros((N, N), ml_dtypes.bfloat16)
    flip[np.arange(N), -np.arange(N) % N] = 1
    planes = np.zeros((128, 128), ml_dtypes.bfloat16)
    for block in range(0, 128, HALF):
        for at in range(1, HALF):
            planes[block + at, block + HALF - at] = 1
    return flip, planes


def split(value):
    high = value.astype(BF)
    low = (value - high.astype(jnp.float32)).astype(BF)
    return high, low


def dot(left, right):
    return jnp.dot(left, right, preferred_element_type=jnp.float32)


def dot3(left_high, left_low, right_high, right_low):
    return dot(left_high, right_high) + (dot(left_high, right_low) + dot(left_low, right_high))


def rotated(value, sign):
    lane = lax.broadcasted_iota(jnp.int32, value.shape, 1)
    swapped = pltpu.roll(value, 64, 1)
    return jnp.where(lane < 64, sign * swapped, -sign * swapped)


def fold(value):
    rows, cols = value.shape
    total = jnp.sum(value.reshape(rows // 8, 8, cols), axis=0)
    parts = [total[:, at : at + 128] for at in range(0, cols, 128)]
    return sum(parts[1:], parts[0])


def lanes(value):
    return lax.broadcasted_iota(jnp.int32, value.shape, value.ndim - 1)


def roll(value, shift):
    shift = shift % 128
    return value if shift == 0 else pltpu.roll(value, shift, value.ndim - 1)


def exchange(first, second):
    even = (lanes(first) & HALF) == 0
    low = jnp.where(even, first, roll(second, HALF))
    high = jnp.where(even, roll(first, -HALF), second)
    return low, high


def complex_dot(table_high, table_low, tiles, sign):
    real = jnp.concatenate(tiles, axis=1)
    turned = jnp.concatenate([rotated(tile, sign) for tile in tiles], axis=1)
    data_high, data_low = split(jnp.concatenate([real, turned], axis=0))
    return dot3(table_high[...], table_low[...], data_high, data_low)


def z_forward_kernel(volume, prior, high, low, out, partial):
    field = volume[...]
    partial[...] = fold((prior[...] * field * field).reshape(M, M))
    rows = jnp.concatenate([volume[:, y, :] for y in range(8)], axis=0)
    rows_high, rows_low = split(rows)
    res = dot3(rows_high, rows_low, high[...], low[...])
    for pair in range(GX // 2):
        tile = res[:, pair * 128 : pair * 128 + 128]
        first, second = exchange(tile[:128], tile[128:])
        out[2 * pair, :128] = first
        out[2 * pair + 1, :128] = second
    edge = res[:, GX * 64 :]
    lane = lax.broadcasted_iota(jnp.int32, (32, 128), 1)
    planes = jnp.zeros((32, 128), jnp.float32)
    for y in range(8):
        planes = jnp.where(lane % 8 == y, edge[y * 32 : y * 32 + 32], planes)
    lane = lax.broadcasted_iota(jnp.int32, (8, 128), 1)
    for block in range(GX):
        tile = jnp.zeros((8, 128), jnp.float32)
        for quarter in range(4):
            moved = roll(planes[quarter * 8 : quarter * 8 + 8], 16 * quarter - 16 * block)
            tile = jnp.where(lane // 16 == quarter, moved, tile)
        out[block, 128:] = tile


def x_forward_kernel(received, held, high, low, out):
    for pair in range(2):
        tiles = [
            received[:, y * 32 : y * 32 + 32, :].reshape(M, 128) for y in (2 * pair, 2 * pair + 1)
        ]
        res = complex_dot(high, low, tiles, 1.0)
        for at in range(2):
            blocks = res[:, at * 128 : at * 128 + 128].reshape(GA, 2, 8, 128)
            first, second = exchange(blocks[:, 0].reshape(M, 128), blocks[:, 1].reshape(M, 128))
            out[:, 2 * pair + at] = first.reshape(GA, 8, 128)
            out[:, 2 * pair + at + 4] = second.reshape(GA, 8, 128)
    lane = lax.broadcasted_iota(jnp.int32, (8, 128), 1)
    rows = []
    for block in range(GX):
        tile = received[block, 128:, :]
        for quarter in range(4):
            real = roll(tile, -16 * quarter)
            imag = roll(tile, 56 - 16 * quarter)
            rows.append(jnp.where(lane < 64, real, imag))
    res = complex_dot(high, low, [jnp.concatenate(rows, axis=0)], 1.0).T
    for group in range(GA):
        cols = slice(group // 8 * 128, group // 8 * 128 + 128)
        shift = -16 * (group % 8)
        out[group, 8] = jnp.where(
            lane < 64, roll(res[0:8, cols], shift), roll(res[64:72, cols], shift + 64)
        )


def doubled(tile):
    first, second = tile[:, :64], tile[:, 64:]
    return jnp.concatenate([first, first, second, second], axis=1)


def pair_order(pair):
    return 2 * pair, 2 * pair + 8, 2 * pair + 1, 2 * pair + 9


def flipped(rows, flip, planes):
    high, low = split(rows)
    turned_high, turned_low = split(dot(planes, high) + dot(planes, low))
    contract = (((1,), (1,)), ((), ()))
    return lax.dot_general(
        flip, turned_high, contract, preferred_element_type=jnp.float32
    ) + lax.dot_general(flip, turned_low, contract, preferred_element_type=jnp.float32)


def pack_kernel(plane, after, other, out):
    for k in range(EARLY + 1, 16):
        out[k - EARLY - 1] = plane[15 - k]


def own_kernel(own, after, out):
    for pair in range(4):
        rows = jnp.concatenate([own[k, :HALF] for k in pair_order(pair)], axis=0)
        out[:, pair * 256 : pair * 256 + 256] = doubled(rows.T)
    edge = jnp.concatenate([own[:, HALF, :], jnp.zeros((48, N), jnp.float32)] * 2, axis=0)
    out[:, 1024:] = edge.T


def near_kernel(base, near, rim, flip, planes, out):
    blank = jnp.zeros((HALF, N), jnp.float32)
    out[...] = base[...]
    for pair in range((EARLY + 2) // 2):
        place = slice(pair * 256, pair * 256 + 256)
        rows = [
            rim[0] if k == 0 else near[EARLY - k] if k <= EARLY else blank for k in pair_order(pair)
        ]
        out[:, place] += doubled(flipped(jnp.concatenate(rows, axis=0), flip[...], planes[...]))


def y_forward_kernel(received, high, low, out):
    for pair in range(4):
        tiles = []
        for at in range(2):
            rows = [
                received[pl.ds(group * 72 + pair * 2 + at, 8, stride=8), :] for group in range(GA)
            ]
            tiles.append(jnp.concatenate(rows, axis=0))
        out[:, pair * 256 : pair * 256 + 256] = complex_dot(high, low, tiles, 1.0)
    rows = [received[group * 72 + 64 : group * 72 + 72, :] for group in range(GA)]
    out[:, 1024:] = complex_dot(high, low, [jnp.concatenate(rows, axis=0)], 1.0)


def y_inverse_kernel(spectrum, base, far, partial, flip, planes, high, low, out):
    blank = jnp.zeros((HALF, N), jnp.float32)

    def mirrored(k):
        return far[k - EARLY - 1] if k > EARLY else blank

    total = partial[...]
    for pair in range(5):
        place = slice(pair * 256, min(pair * 256 + 256, 1152))
        scale = base[:, place]
        if pair < 4:
            rows = jnp.concatenate([mirrored(k) for k in pair_order(pair)], axis=0)
            scale += doubled(flipped(rows, flip[...], planes[...]))
        values = spectrum[:, place]
        weighted = values * scale
        total += fold(weighted * values) * (1.0 / float(N) ** 3)
        cols = [weighted[:, at : at + 128] for at in range(0, values.shape[1], 128)]
        res = complex_dot(high, low, cols, -1.0)
        if pair == 4:
            res = jnp.where(lanes(res) < 96, res, jnp.sum(total))
        out[:, :, place] = res.reshape(GA, 8, res.shape[1])


def x_inverse_kernel(received, high, low, plain_high, plain_low, out):
    for pair in range(2):
        tiles = []
        for y in (2 * pair, 2 * pair + 1):
            first, second = (
                jnp.concatenate(
                    [received[:, at, k * 128 : k * 128 + 128] for k in range(8)], axis=0
                )
                for at in (y, y + 4)
            )
            tiles.append(jnp.concatenate(exchange(first, second), axis=0))
        res = complex_dot(high, low, tiles, -1.0)
        for at in range(2):
            y = 2 * pair + at
            out[:, y * 32 : y * 32 + 32, :] = res[:, at * 128 : at * 128 + 128].reshape(GX, 32, 128)
    lane = lax.broadcasted_iota(jnp.int32, (8, 128), 1)
    real, imag = [], []
    count = jnp.zeros((1, 1), jnp.float32)
    for four in range(4):
        real_tile = jnp.zeros((8, 128), jnp.float32)
        imag_tile = real_tile
        for at in range(8):
            tile = received[four * 8 + at, :, 1024:]
            count += tile[:1, 127:]
            here = lane // 16 == at
            real_tile = jnp.where(here, roll(tile, 16 * at), real_tile)
            imag_tile = jnp.where(here, roll(tile, 16 * at - 64), imag_tile)
        real.append(real_tile)
        imag.append(imag_tile)
    blank = jnp.zeros((56, N), jnp.float32)
    stacked = jnp.concatenate(
        [jnp.concatenate(real, axis=1), blank, jnp.concatenate(imag, axis=1), blank], axis=0
    )
    res = complex_dot(plain_high, plain_low, [stacked.T], -1.0)
    for block in range(GX):
        tile = jnp.broadcast_to(count, (8, 128))
        for quarter in range(4):
            part = res[block * 32 + quarter * 8 : block * 32 + quarter * 8 + 8]
            tile = jnp.where(lane // 8 == 2 * quarter, roll(part, 16 * quarter), tile)
            tile = jnp.where(lane // 8 == 2 * quarter + 1, roll(part, 16 * quarter - 56), tile)
        out[block, 128:] = tile


def z_inverse_kernel(received, volume, prior, high, low, out, curvature):
    lower, upper = [], []
    for pair in range(GX // 2):
        first, second = exchange(received[2 * pair, :128], received[2 * pair + 1, :128])
        lower.append(first)
        upper.append(second)
    lane = lax.broadcasted_iota(jnp.int32, (8, 128), 1)
    planes = []
    for quarter in range(4):
        tile = jnp.zeros((8, 128), jnp.float32)
        for block in range(GX):
            moved = roll(received[block, 128:], 16 * block - 16 * quarter)
            tile = jnp.where(lane // 16 == block, moved, tile)
        planes.append(tile)
    planes = jnp.concatenate(planes, axis=0)
    edge = jnp.concatenate(
        [jnp.where(lanes(planes) % 8 == y, planes, 0.0) for y in range(8)], axis=0
    )
    main = jnp.concatenate(
        [jnp.concatenate(lower, axis=1), jnp.concatenate(upper, axis=1)], axis=0
    )
    data_high, data_low = split(jnp.concatenate([main, edge], axis=1))
    image = dot3(data_high, data_low, high[...], low[...])
    for y in range(8):
        out[:, y, :] = image[y * 32 : y * 32 + 32, :] + prior[:, y, :] * volume[:, y, :]
    total = jnp.sum(received[:, 128:, 127:].reshape(GX * 8, 1)) / 8.0
    curvature[0] = total / float(M) ** 3


def whole():
    return pl.BlockSpec(memory_space=pltpu.VMEM)


def params():
    return pltpu.CompilerParams(vmem_limit_bytes=VMEM_LIMIT)


def cost(micros):
    return pl.CostEstimate(flops=int(micros * 1e9), bytes_accessed=8 << 20, transcendentals=0)


def f32(*shape):
    return jax.ShapeDtypeStruct(shape, jnp.float32)


def mirror(value, shift):
    pairs = [((shift - group) % GA, group) for group in range(GA)]
    return lax.ppermute(value, ("gy", "gz"), pairs)


def opposite(value):
    return lax.ppermute(value, "gx", [(GX - 1 - block, block) for block in range(GX)])


def local(volume, prior_weight, kernel):
    flips = flip_tables()
    turned = opposite(kernel[16 - EARLY :, HALF:])
    near = mirror(turned, 31)
    plane = mirror(kernel[1 : 16 - EARLY, HALF:], 31)
    rim = opposite(mirror(kernel[:1, HALF:], 32))
    base = pl.pallas_call(
        own_kernel,
        out_shape=f32(N, 1152),
        in_specs=[whole(), pl.BlockSpec(memory_space=pl.ANY)],
        out_specs=whole(),
        compiler_params=params(),
        cost_estimate=cost(OWN_COST),
        name="own_weights",
    )(kernel, turned)
    sent, partial = pl.pallas_call(
        z_forward_kernel,
        out_shape=(f32(GX, 136, 128), f32(8, 128)),
        in_specs=[whole()] * 4,
        out_specs=(whole(), whole()),
        compiler_params=params(),
        name="z_forward",
    )(volume, prior_weight, *z_forward_table())
    got = lax.all_to_all(sent, "gx", split_axis=0, concat_axis=0, tiled=True)
    packed = pl.pallas_call(
        pack_kernel,
        out_shape=f32(15 - EARLY, HALF, N),
        in_specs=[whole()] + [pl.BlockSpec(memory_space=pl.ANY)] * 2,
        out_specs=whole(),
        compiler_params=params(),
        cost_estimate=cost(PACK_COST),
        name="pack",
    )(plane, got, base)
    far = opposite(packed)
    sent = pl.pallas_call(
        x_forward_kernel,
        out_shape=f32(GA, 9, 8, 128),
        in_specs=[whole(), pl.BlockSpec(memory_space=pl.ANY), whole(), whole()],
        out_specs=whole(),
        compiler_params=params(),
        name="x_forward",
    )(got, packed, *forward_table())
    got = lax.all_to_all(sent, ("gy", "gz"), split_axis=0, concat_axis=0, tiled=True)
    base = pl.pallas_call(
        near_kernel,
        out_shape=f32(N, 1152),
        in_specs=[whole()] * 5,
        out_specs=whole(),
        compiler_params=params(),
        cost_estimate=cost(NEAR_COST),
        name="near_weights",
    )(base, near, rim, *flips)
    spectrum = pl.pallas_call(
        y_forward_kernel,
        out_shape=f32(N, 1152),
        in_specs=[whole()] * 3,
        out_specs=whole(),
        compiler_params=params(),
        cost_estimate=cost(FORWARD_COST),
        name="y_forward",
    )(got.reshape(GA * 72, 128), *forward_table())
    sent = pl.pallas_call(
        y_inverse_kernel,
        out_shape=f32(GA, 8, 1152),
        in_specs=[whole()] * 8,
        out_specs=whole(),
        compiler_params=params(),
        name="y_inverse",
    )(spectrum, base, far, partial, *flips, *inverse_table())
    got = lax.all_to_all(sent, ("gy", "gz"), split_axis=0, concat_axis=0, tiled=True)
    sent = pl.pallas_call(
        x_inverse_kernel,
        out_shape=f32(GX, 136, 128),
        in_specs=[whole()] * 5,
        out_specs=whole(),
        compiler_params=params(),
        name="x_inverse",
    )(got, *x_inverse_table(), *inverse_table())
    got = lax.all_to_all(sent, "gx", split_axis=0, concat_axis=0, tiled=True)
    product, curvature = pl.pallas_call(
        z_inverse_kernel,
        out_shape=(f32(32, 8, M), f32(1)),
        in_specs=[whole()] * 5,
        out_specs=(whole(), pl.BlockSpec(memory_space=pltpu.SMEM)),
        compiler_params=params(),
        name="z_inverse",
    )(got, volume, prior_weight, *z_inverse_table())
    return product, curvature


def solution(mesh):
    return jax.shard_map(
        local,
        mesh=mesh,
        in_specs=(
            P("gx", ("gy", "gz"), None),
            P("gx", ("gy", "gz"), None),
            P(("gy", "gz"), "gx", None),
        ),
        out_specs=(P("gx", ("gy", "gz"), None), P()),
        check_vma=False,
    )
```

time: 177 us -> 140 us (0.79)
  blocking collectives: 143 us -> 45.7 us
  starting transfers between devices: 0 us -> 37 us
  waiting for transfers between devices: 0 us -> 20.3 us
  local copies, waits for them, and re-layouts: 4.63 us -> 11.5 us
  Pallas kernels: 28.2 us -> 23.6 us
    all_to_all x2 -> x1, blocking collectives: 74.5 us -> 22.7 us  [local(): lax.all_to_all(sent, ('gy', 'gz'), split_axis=0, concat_axis=0, tiled=True)]
    all_to_all x2 -> x1, blocking collectives: 68.1 us -> 23 us  [local(): got = lax.all_to_all(sent, 'gx', split_axis=0, concat_axis=0, tiled=True)]
    ppermute x0 -> x6, starting transfers between devices: none -> 26.1 us  [the longest x3 13.9 us: mirror(): return lax.ppermute(value, ('gy', 'gz'), pairs)]
    all_to_all x0 -> x2, waiting for transfers between devices: none -> 13.9 us  [the longest x1 13.9 us: local(): lax.all_to_all(sent, ('gy', 'gz'), split_axis=0, concat_axis=0, tiled=True)]
    all_to_all x0 -> x2, starting transfers between devices: none -> 11 us  [the longest x1 7.43 us: local(): lax.all_to_all(sent, ('gy', 'gz'), split_axis=0, concat_axis=0, tiled=True)]
    ppermute x0 -> x6, waiting for transfers between devices: none -> 6.36 us  [the longest x3 6.35 us: mirror(): return lax.ppermute(value, ('gy', 'gz'), pairs)]
    unnamed x28 -> x44, local copies, waits for them, and re-layouts: 4.12 us -> 10.4 us
    pallas_call x5 -> x9, Pallas kernels: 28.2 us -> 23.6 us  [the longest x1 6.76 us: local(): pl.pallas_call(y_inverse_kernel, out_shape=f32(GA, 8, 1152), in_specs=[wh...]
  transfers between devices with their start and end apart: 0 -> 8, of which waited for: 0 -> 2; matrix products, arithmetic and copies ran while one was open for 0% -> 0% of each run, Pallas kernels for 0% -> 10%
where the time goes in v1:
time: 140 us; the launch traced here: 139 us
  blocking collectives  45.7 us (33%)
  starting transfers between devices  37 us (26%)
  Pallas kernels  23.6 us (17%)
  waiting for transfers between devices  20.3 us (14%)
  local copies, waits for them, and re-layouts  11.5 us (8%)
    all_to_all x1, blocking collectives, local(): got = lax.all_to_all(sent, 'gx', split_axis=0, concat_axis=0, tiled=True)  23 us
    all_to_all x1, blocking collectives, local(): lax.all_to_all(sent, ('gy', 'gz'), split_axis=0, concat_axis=0, tiled=True)  22.7 us
    all_to_all x1, waiting for transfers between devices, local(): lax.all_to_all(sent, ('gy', 'gz'), split_axis=0, concat_axis=0, tiled=True)  13.9 us
    ppermute x3, starting transfers between devices, mirror(): return lax.ppermute(value, ('gy', 'gz'), pairs)  13.9 us
    ppermute x3, starting transfers between devices, opposite(): lax.ppermute(value, 'gx', [(GX - 1 - block, block) for block in range(GX)])  12.2 us
    unnamed x44, local copies, waits for them, and re-layouts  10.4 us
    all_to_all x1, starting transfers between devices, local(): lax.all_to_all(sent, ('gy', 'gz'), split_axis=0, concat_axis=0, tiled=True)  7.43 us
    pallas_call x1, Pallas kernels, local(): pl.pallas_call(y_inverse_kernel, out_shape=f32(GA, 8, 1152), in_specs=[wh...  6.76 us
  transfers between devices with their start and end apart: 8, of which 2 were waited for; matrix products, arithmetic and copies ran while one was open for 0% of the time, Pallas kernels for 10%

profile of v1, /device:TPU:1, one launch (start us, length us, event | category | flops | bytes accessed | tf_op | source)
XLA Modules:
  0.0 139.0 jit_solution(7811562038312377954)
XLA Ops:
  0.6 1.0 slice.10
  1.6 6.5 %collective-permute-start.1 = (f32[4,32,512]{2,1,0:T(8,128)S(1)}, f32[4,32,512]{2,1,0:T(8,128)S(1)}, u32[]{:S(2)}, u32[]{:S(2)}) collective-permute-start(f32[4,32,512]{2,1,0:T(8,128)S(1)} %slice.10), channel_id=1, source_target_pairs={{224,0},{192,32},{160,64},{128,96},{96,128},{64,160},{32,192},{0,2... | collective-permute-start | bytes 786440 | tf_op jit(solution)/shard_map/ppermute | solution.py:357
  8.1 0.9 copy-done.3
  9.1 0.9 copy-done.5
  10.0 1.0 copy-done.15
  11.0 1.0 copy-done.16
  11.9 1.5 %z_forward.1 = (f32[8,136,128]{2,1,0:T(8,128)}, f32[8,128]{1,0:T(8,128)S(1)}) custom-call(f32[32,8,256]{2,1,0:T(8,128)S(1)} %copy-done.3, f32[32,8,256]{2,1,0:T(8,128)S(1)} %copy-done.5, bf16[256,640]{1,0:T(8,128)(2,1)S(1)} %copy-done.16, bf16[256,640]{1,0:T(8,128)(2,1)S(1)} %copy-done.15), custom_call_target="tpu_custom_call" | custom-call | tf_op jit(solution)/shard_map/z_forward/pallas_call | solution.py:375
  13.4 3.5 %all-to-all-start = ((f32[8,136,128]{2,1,0:T(8,128)}), f32[8,136,128]{2,1,0:T(8,128)S(1)}, u32[]{:S(2)}, u32[]{:S(2)}) async-start(f32[8,136,128]{2,1,0:T(8,128)} %get-tuple-element.4), calls=%async_computation | async-start | bytes 1114112 | tf_op jit(solution)/shard_map/all_to_all | solution.py:383
  17.0 3.1 %collective-permute-start.3 = (f32[1,32,512]{2,1,0:T(8,128)S(1)}, f32[1,32,512]{2,1,0:T(8,128)}, u32[]{:S(2)}, u32[]{:S(2)}) collective-permute-start(f32[1,32,512]{2,1,0:T(8,128)S(1)} %slice.11), channel_id=1, source_target_pairs={{0,0},{31,1},{30,2},{29,3},{28,4},{27,5},{26,6},{25,7},{24,8},{23,... | collective-permute-start | bytes 196616 | tf_op jit(solution)/shard_map/ppermute | solution.py:353
  20.1 0.1 slice.9
  20.2 4.7 %collective-permute-start = (f32[11,32,512]{2,1,0:T(8,128)S(1)}, f32[11,32,512]{2,1,0:T(8,128)S(1)}, u32[]{:S(2)}, u32[]{:S(2)}) collective-permute-start(f32[11,32,512]{2,1,0:T(8,128)S(1)} %slice.9), channel_id=1, source_target_pairs={{31,0},{30,1},{29,2},{28,3},{27,4},{26,5},{25,6},{24,7},{23,8},{22... | collective-permute-start | bytes 2162696 | tf_op jit(solution)/shard_map/ppermute | solution.py:353
  24.9 2.9 %collective-permute-start.4 = (f32[1,32,512]{2,1,0:T(8,128)}, f32[1,32,512]{2,1,0:T(8,128)S(1)}, u32[]{:S(2)}, u32[]{:S(2)}) collective-permute-start(f32[1,32,512]{2,1,0:T(8,128)} %collective-permute-done.3), channel_id=1, source_target_pairs={{224,0},{192,32},{160,64},{128,96},{96,128},{64,160},{32,192},{0,2... | collective-permute-start | bytes 196616 | tf_op jit(solution)/shard_map/ppermute | solution.py:357
  27.9 6.0 %collective-permute-start.2 = (f32[4,32,512]{2,1,0:T(8,128)S(1)}, f32[4,32,512]{2,1,0:T(8,128)}, u32[]{:S(2)}, u32[]{:S(2)}) collective-permute-start(f32[4,32,512]{2,1,0:T(8,128)S(1)} %collective-permute-done.1.after), channel_id=1, source_target_pairs={{31,0},{30,1},{29,2},{28,3},{27,4},{26,5},{25,6},{24,7},{23,8},{22... | collective-permute-start | bytes 786440 | tf_op jit(solution)/shard_map/ppermute | solution.py:353
  33.9 2.1 %own_weights.1.other.base = f32[512,1152]{1,0:T(8,128)} custom-call(f32[16,64,512]{2,1,0:T(8,128)S(1)} %copy-done.8, f32[4,32,512]{2,1,0:T(8,128)S(1)} %collective-permute-done.1.after), custom_call_target="tpu_custom_call" | custom-call | flops 8000000000 | bytes 8388608 | tf_op jit(solution)/shard_map/own_weights/pallas_call | solution.py:366
  36.0 6.3 %collective-permute-done.plane = f32[11,32,512]{2,1,0:T(8,128)S(1)} collective-permute-done((f32[11,32,512]{2,1,0:T(8,128)S(1)}, f32[11,32,512]{2,1,0:T(8,128)S(1)}, u32[]{:S(2)}, u32[]{:S(2)}) %collective-permute-start) | collective-permute-done | bytes 720928 | tf_op jit(solution)/shard_map/ppermute | solution.py:353
  42.4 0.9 copy-done.20
  43.2 1.1 copy-done.21
  44.4 2.8 %collective-permute-start.5 = (f32[11,32,512]{2,1,0:T(8,128)S(1)}, f32[11,32,512]{2,1,0:T(8,128)S(1)}, u32[]{:S(2)}, u32[]{:S(2)}) collective-permute-start(f32[11,32,512]{2,1,0:T(8,128)S(1)} %pack.1.held), channel_id=1, source_target_pairs={{224,0},{192,32},{160,64},{128,96},{96,128},{64,160},{32,192},{0,2... | collective-permute-start | bytes 2162696 | tf_op jit(solution)/shard_map/ppermute | solution.py:357
  47.2 1.0 copy-done.11
  48.2 2.7 %x_forward.1 = f32[32,9,8,128]{3,2,1,0:T(8,128)} custom-call(f32[8,136,128]{2,1,0:T(8,128)S(1)} %all-to-all-done.after.received, f32[11,32,512]{2,1,0:T(8,128)S(1)} %pack.1.held, bf16[512,512]{1,0:T(8,128)(2,1)S(1)} %copy-done.11, bf16[512,512]{1,0:T(8,128)(2,1)S(1)} %copy-done.9), custom_call_target="tpu_custom_call" | custom-call | tf_op jit(solution)/shard_map/x_forward/pallas_call | solution.py:394
  50.9 7.4 %all-to-all-start.1 = ((f32[32,9,8,128]{3,2,1,0:T(8,128)}), f32[32,9,8,128]{3,2,1,0:T(8,128)S(1)}, u32[]{:S(2)}, u32[]{:S(2)}) async-start(f32[32,9,8,128]{3,2,1,0:T(8,128)} %x_forward.1), calls=%async_computation.1 | async-start | bytes 2359296 | tf_op jit(solution)/shard_map/all_to_all | solution.py:402
  58.4 3.2 %near_weights.1.base = f32[512,1152]{1,0:T(8,128)S(1)} custom-call(f32[512,1152]{1,0:T(8,128)} %own_weights.1.other.base, f32[4,32,512]{2,1,0:T(8,128)} %collective-permute-done.2.near, f32[1,32,512]{2,1,0:T(8,128)S(1)} %collective-permute-done.4.rim, bf16[512,512]{1,0:T(8,128)(2,1)S(1)} %copy-done.7, bf16[128,128]{1,0:T(8,128)(2,1)S(1)} %copy-done.19), custom_call_target="tpu_custom_call" | custom-call | flops 20000000000 | bytes 8388608 | tf_op jit(solution)/shard_map/near_weights/pallas_call | solution.py:403
  61.6 1.4 %copy-done = f32[512,1152]{1,0:T(8,128)} copy-done((f32[512,1152]{1,0:T(8,128)}, f32[512,1152]{1,0:T(8,128)S(1)}, u32[]{:S(2)}) %copy-start) | copy-done | bytes 2359320
  63.0 13.9 %all-to-all-done.1 = f32[32,9,8,128]{3,2,1,0:T(8,128)S(1)} async-done(((f32[32,9,8,128]{3,2,1,0:T(8,128)}), f32[32,9,8,128]{3,2,1,0:T(8,128)S(1)}, u32[]{:S(2)}, u32[]{:S(2)}) %all-to-all-start.1) | async-done | bytes 1179680 | tf_op jit(solution)/shard_map/all_to_all | solution.py:402
  76.9 1.0 copy-done.10
  78.0 1.0 copy-done.12
  79.0 3.8 %y_forward.1.spectrum = f32[512,1152]{1,0:T(8,128)} custom-call(f32[2304,128]{1,0:T(8,128)S(1)} %bitcast.1, bf16[512,512]{1,0:T(8,128)(2,1)S(1)} %copy-done.12, bf16[512,512]{1,0:T(8,128)(2,1)S(1)} %copy-done.10), custom_call_target="tpu_custom_call" | custom-call | flops 5000000000 | bytes 8388608 | tf_op jit(solution)/shard_map/y_forward/pallas_call | solution.py:412
  82.8 6.8 %y_inverse.1 = f32[32,8,1152]{2,1,0:T(8,128)S(1)} custom-call(f32[512,1152]{1,0:T(8,128)} %y_forward.1.spectrum, f32[512,1152]{1,0:T(8,128)} %copy-done, f32[11,32,512]{2,1,0:T(8,128)S(1)} %collective-permute-done.5.far, f32[8,128]{1,0:T(8,128)S(1)} %get-tuple-element.5.partial, bf16[512,512]{1,0:T(8,128)(2,1)S(1)} %copy-done.7, ...), custom_call_target="tpu_custom_call" | custom-call | tf_op jit(solution)/shard_map/y_inverse/pallas_call | solution.py:421
  89.6 22.7 %all_to_all.20.received = f32[32,8,1152]{2,1,0:T(8,128)S(1)} all-to-all(f32[32,8,1152]{2,1,0:T(8,128)S(1)} %y_inverse.1), channel_id=1, replica_groups=mesh['gx'=8,'gy'=4,'gz'=8] {'gy','gz'}, dimensions={0} | all-to-all | bytes 2359296 | tf_op jit(solution)/shard_map/all_to_all | solution.py:429
  112.4 2.1 %x_inverse.1 = f32[8,136,128]{2,1,0:T(8,128)S(1)} custom-call(f32[32,8,1152]{2,1,0:T(8,128)S(1)} %all_to_all.20.received, bf16[256,1024]{1,0:T(8,128)(2,1)S(1)} %copy-done.14, bf16[256,1024]{1,0:T(8,128)(2,1)S(1)} %copy-done.13, bf16[256,1024]{1,0:T(8,128)(2,1)S(1)} %copy-done.2, bf16[256,1024]{1,0:T(8,128)(2,1)S(1)} %copy-done.1), custom_call_target="tpu_custom_call" | custom-call | tf_op jit(solution)/shard_map/x_inverse/pallas_call | solution.py:430
  114.5 23.0 %all_to_all.21.received = f32[8,136,128]{2,1,0:T(8,128)S(1)} all-to-all(f32[8,136,128]{2,1,0:T(8,128)S(1)} %x_inverse.1), channel_id=1, replica_groups=mesh['gx'=8,'gy'=4,'gz'=8] {'gx'}, dimensions={0} | all-to-all | bytes 1114112 | tf_op jit(solution)/shard_map/all_to_all | solution.py:438
  137.5 1.4 %z_inverse.1 = (f32[32,8,256]{2,1,0:T(8,128)}, f32[1]{0:T(128)}) custom-call(f32[8,136,128]{2,1,0:T(8,128)S(1)} %all_to_all.21.received, f32[32,8,256]{2,1,0:T(8,128)S(1)} %copy-done.4, f32[32,8,256]{2,1,0:T(8,128)S(1)} %copy-done.6, bf16[640,256]{1,0:T(8,128)(2,1)S(1)} %copy-done.18, bf16[640,256]{1,0:T(8,128)(2,1)S(1)} %copy-done.17), custom_call_target="tpu_custom_call" | custom-call | tf_op jit(solution)/shard_map/z_inverse/pallas_call | solution.py:439
  (42 shorter events, 0.1 us)
Async XLA Ops:
  1.6 26.3 %collective-permute-start.1 = (f32[4,32,512]{2,1,0:T(8,128)S(1)}, f32[4,32,512]{2,1,0:T(8,128)S(1)}, u32[]{:S(2)}, u32[]{:S(2)}) collective-permute-start(f32[4,32,512]{2,1,0:T(8,128)S(1)} %slice.10), channel_id=1, source_target_pairs={{224,0},{192,32},{160,64},{128,96},{96,128},{64,160},{32,192},{0,2... | collective-permute-start | bytes 786440 | tf_op jit(solution)/shard_map/ppermute | solution.py:357
  8.1 0.9 copy-start.3
  9.1 0.9 copy-start.5
  10.0 1.0 copy-start.15
  11.0 1.0 copy-start.16
  11.9 5.0 %copy-start.8 = (f32[16,64,512]{2,1,0:T(8,128)S(1)}, f32[16,64,512]{2,1,0:T(8,128)}, u32[]{:S(2)}) copy-start(f32[16,64,512]{2,1,0:T(8,128)} %own.1) | copy-start | bytes 6291460
  13.4 29.8 %all-to-all-start = ((f32[8,136,128]{2,1,0:T(8,128)}), f32[8,136,128]{2,1,0:T(8,128)S(1)}, u32[]{:S(2)}, u32[]{:S(2)}) async-start(f32[8,136,128]{2,1,0:T(8,128)} %get-tuple-element.4), calls=%async_computation | async-start | bytes 1114112 | tf_op jit(solution)/shard_map/all_to_all | solution.py:383
  17.0 7.9 %collective-permute-start.3 = (f32[1,32,512]{2,1,0:T(8,128)S(1)}, f32[1,32,512]{2,1,0:T(8,128)}, u32[]{:S(2)}, u32[]{:S(2)}) collective-permute-start(f32[1,32,512]{2,1,0:T(8,128)S(1)} %slice.11), channel_id=1, source_target_pairs={{0,0},{31,1},{30,2},{29,3},{28,4},{27,5},{26,6},{25,7},{24,8},{23,... | collective-permute-start | bytes 196616 | tf_op jit(solution)/shard_map/ppermute | solution.py:353
  20.2 22.2 %collective-permute-start = (f32[11,32,512]{2,1,0:T(8,128)S(1)}, f32[11,32,512]{2,1,0:T(8,128)S(1)}, u32[]{:S(2)}, u32[]{:S(2)}) collective-permute-start(f32[11,32,512]{2,1,0:T(8,128)S(1)} %slice.9), channel_id=1, source_target_pairs={{31,0},{30,1},{29,2},{28,3},{27,4},{26,5},{25,6},{24,7},{23,8},{22... | collective-permute-start | bytes 2162696 | tf_op jit(solution)/shard_map/ppermute | solution.py:353
  24.9 33.4 %collective-permute-start.4 = (f32[1,32,512]{2,1,0:T(8,128)}, f32[1,32,512]{2,1,0:T(8,128)S(1)}, u32[]{:S(2)}, u32[]{:S(2)}) collective-permute-start(f32[1,32,512]{2,1,0:T(8,128)} %collective-permute-done.3), channel_id=1, source_target_pairs={{224,0},{192,32},{160,64},{128,96},{96,128},{64,160},{32,192},{0,2... | collective-permute-start | bytes 196616 | tf_op jit(solution)/shard_map/ppermute | solution.py:357
  27.9 30.5 %collective-permute-start.2 = (f32[4,32,512]{2,1,0:T(8,128)S(1)}, f32[4,32,512]{2,1,0:T(8,128)}, u32[]{:S(2)}, u32[]{:S(2)}) collective-permute-start(f32[4,32,512]{2,1,0:T(8,128)S(1)} %collective-permute-done.1.after), channel_id=1, source_target_pairs={{31,0},{30,1},{29,2},{28,3},{27,4},{26,5},{25,6},{24,7},{23,8},{22... | collective-permute-start | bytes 786440 | tf_op jit(solution)/shard_map/ppermute | solution.py:353
  36.0 11.2 %copy-start.9 = (bf16[512,512]{1,0:T(8,128)(2,1)S(1)}, bf16[512,512]{1,0:T(8,128)(2,1)}, u32[]{:S(2)}) copy-start(bf16[512,512]{1,0:T(8,128)(2,1)} %constant.27.clone.low) | copy-start | bytes 1572868
  42.4 0.9 copy-start.20
  43.2 1.1 copy-start.21
  44.4 14.0 %copy-start.7 = (bf16[512,512]{1,0:T(8,128)(2,1)S(1)}, bf16[512,512]{1,0:T(8,128)(2,1)}, u32[]{:S(2)}) copy-start(bf16[512,512]{1,0:T(8,128)(2,1)} %constant.28.clone.flip) | copy-start | bytes 1572868
  44.4 38.4 %collective-permute-start.5 = (f32[11,32,512]{2,1,0:T(8,128)S(1)}, f32[11,32,512]{2,1,0:T(8,128)S(1)}, u32[]{:S(2)}, u32[]{:S(2)}) collective-permute-start(f32[11,32,512]{2,1,0:T(8,128)S(1)} %pack.1.held), channel_id=1, source_target_pairs={{224,0},{192,32},{160,64},{128,96},{96,128},{64,160},{32,192},{0,2... | collective-permute-start | bytes 2162696 | tf_op jit(solution)/shard_map/ppermute | solution.py:357
  47.2 1.0 copy-start.11
  48.2 10.2 %copy-start.19 = (bf16[128,128]{1,0:T(8,128)(2,1)S(1)}, bf16[128,128]{1,0:T(8,128)(2,1)}, u32[]{:S(2)}) copy-start(bf16[128,128]{1,0:T(8,128)(2,1)} %constant.29.clone.planes) | copy-start | bytes 98308
  50.9 26.0 %all-to-all-start.1 = ((f32[32,9,8,128]{3,2,1,0:T(8,128)}), f32[32,9,8,128]{3,2,1,0:T(8,128)S(1)}, u32[]{:S(2)}, u32[]{:S(2)}) async-start(f32[32,9,8,128]{3,2,1,0:T(8,128)} %x_forward.1), calls=%async_computation.1 | async-start | bytes 2359296 | tf_op jit(solution)/shard_map/all_to_all | solution.py:402
  61.6 1.4 %copy-start = (f32[512,1152]{1,0:T(8,128)}, f32[512,1152]{1,0:T(8,128)S(1)}, u32[]{:S(2)}) copy-start(f32[512,1152]{1,0:T(8,128)S(1)} %near_weights.1.base) | copy-start | bytes 7077892
  76.9 1.0 copy-start.10
  78.0 1.0 copy-start.12
  79.0 3.8 %copy-start.1 = (bf16[256,1024]{1,0:T(8,128)(2,1)S(1)}, bf16[256,1024]{1,0:T(8,128)(2,1)}, u32[]{:S(2)}) copy-start(bf16[256,1024]{1,0:T(8,128)(2,1)} %constant.31.clone.low.plain_low) | copy-start | bytes 1572868
  79.0 3.8 %copy-start.2 = (bf16[256,1024]{1,0:T(8,128)(2,1)S(1)}, bf16[256,1024]{1,0:T(8,128)(2,1)}, u32[]{:S(2)}) copy-start(bf16[256,1024]{1,0:T(8,128)(2,1)} %constant.30.clone.high.plain_high) | copy-start | bytes 1572868
  89.6 22.8 %copy-start.13 = (bf16[256,1024]{1,0:T(8,128)(2,1)S(1)}, bf16[256,1024]{1,0:T(8,128)(2,1)}, u32[]{:S(2)}) copy-start(bf16[256,1024]{1,0:T(8,128)(2,1)} %constant.33.clone.low) | copy-start | bytes 1572868
  89.6 22.8 %copy-start.14 = (bf16[256,1024]{1,0:T(8,128)(2,1)S(1)}, bf16[256,1024]{1,0:T(8,128)(2,1)}, u32[]{:S(2)}) copy-start(bf16[256,1024]{1,0:T(8,128)(2,1)} %constant.32.clone.high) | copy-start | bytes 1572868
  112.3 25.1 %copy-start.4 = (f32[32,8,256]{2,1,0:T(8,128)S(1)}, f32[32,8,256]{2,1,0:T(8,128)}, u32[]{:S(2)}) copy-start(f32[32,8,256]{2,1,0:T(8,128)} %volume.3) | copy-start | bytes 786436
  112.3 25.1 %copy-start.6 = (f32[32,8,256]{2,1,0:T(8,128)S(1)}, f32[32,8,256]{2,1,0:T(8,128)}, u32[]{:S(2)}) copy-start(f32[32,8,256]{2,1,0:T(8,128)} %prior.3) | copy-start | bytes 786436
  112.3 25.1 %copy-start.17 = (bf16[640,256]{1,0:T(8,128)(2,1)S(1)}, bf16[640,256]{1,0:T(8,128)(2,1)}, u32[]{:S(2)}) copy-start(bf16[640,256]{1,0:T(8,128)(2,1)} %constant.35.clone.low) | copy-start | bytes 983044
  112.4 25.1 %copy-start.18 = (bf16[640,256]{1,0:T(8,128)(2,1)S(1)}, bf16[640,256]{1,0:T(8,128)(2,1)}, u32[]{:S(2)}) copy-start(bf16[640,256]{1,0:T(8,128)(2,1)} %constant.34.clone.high) | copy-start | bytes 983044

commit v2 on v1

v2 whole, which is shorter than its diff:
```python
import math

import jax
import jax.numpy as jnp
import ml_dtypes
import numpy as np
from jax import lax
from jax.experimental import pallas as pl
from jax.experimental.pallas import tpu as pltpu
from jax.sharding import PartitionSpec as P

M = 256
N = 512
GX = 8
GA = 32
HALF = 32
EARLY = 6
LATE = 15 - EARLY
OWN_COST = 20
TURN_COST = 8
FORWARD_COST = 5
AXES = ("gx", "gy", "gz")
VM = 32
BF = jnp.bfloat16


def trig(rows, cols):
    product = np.outer(np.asarray(rows), np.asarray(cols)) % N
    angle = product * (2.0 * math.pi / N)
    return np.cos(angle), np.sin(angle)


def halves(table):
    table = np.asarray(table, np.float32)
    high = table.astype(ml_dtypes.bfloat16)
    low = (table - high.astype(np.float32)).astype(ml_dtypes.bfloat16)
    return high, low


def z_forward_table():
    cosine, sine = trig(np.arange(M), np.arange(N))
    stacked = np.stack([cosine, -sine], axis=0).reshape(2, M, GX // 2, 2, 64)
    main = stacked[..., :HALF].transpose(1, 2, 0, 3, 4).reshape(M, GX * 64)
    edge = stacked[..., HALF].transpose(1, 2, 3, 0).reshape(M, GX * 2)
    return np.concatenate(halves(np.concatenate([main, np.repeat(edge, 8, axis=1)], axis=1)), axis=0)


def z_inverse_table():
    cosine, sine = trig(np.arange(N), np.arange(M))
    stacked = np.stack([cosine, -sine], axis=0).reshape(2, GX // 2, 2, 64, M)
    main = stacked[:, :, :, :HALF].transpose(1, 0, 2, 3, 4).reshape(GX * 64, M)
    edge = stacked[:, :, :, HALF].transpose(1, 2, 0, 3).reshape(GX * 2, M)
    return stack_right(np.concatenate([main, np.repeat(edge, 8, axis=0)], axis=0) / float(N) ** 3)


def forward_table():
    cosine, sine = trig(np.arange(N), np.arange(M))
    return stack_left(np.concatenate([cosine, sine], axis=1))


def inverse_table():
    cosine, sine = trig(np.arange(M), np.arange(N))
    return stack_left(np.concatenate([cosine, sine], axis=1))


def x_inverse_table():
    order = np.arange(N).reshape(GA, 16).T.reshape(-1)
    cosine, sine = trig(np.arange(M), order)
    return stack_left(np.concatenate([cosine, sine], axis=1))


def split(value):
    high = value.astype(BF)
    low = (value - high.astype(jnp.float32)).astype(BF)
    return high, low


def dot(left, right):
    return jnp.dot(left, right, preferred_element_type=jnp.float32)


def stack_left(table):
    return np.concatenate(halves(table), axis=1)


def stack_right(table):
    high, low = halves(table)
    return np.concatenate([high, low, high], axis=0)


def table_dot(table, data):
    high, low = split(data)
    depth = data.shape[0]
    return dot(table[...], jnp.concatenate([high, high], axis=0)) + dot(table[:, :depth], low)


def data_dot(data, table):
    high, low = split(data)
    return dot(jnp.concatenate([high, high, low], axis=1), table[...])


def rotated(value, sign):
    lane = lax.broadcasted_iota(jnp.int32, value.shape, 1)
    swapped = pltpu.roll(value, 64, 1)
    return jnp.where(lane < 64, sign * swapped, -sign * swapped)


def fold(value):
    rows, cols = value.shape
    total = jnp.sum(value.reshape(rows // 8, 8, cols), axis=0)
    parts = [total[:, at : at + 128] for at in range(0, cols, 128)]
    return sum(parts[1:], parts[0])


def lanes(value):
    return lax.broadcasted_iota(jnp.int32, value.shape, value.ndim - 1)


def roll(value, shift):
    shift = shift % 128
    return value if shift == 0 else pltpu.roll(value, shift, value.ndim - 1)


def exchange(first, second):
    even = (lanes(first) & HALF) == 0
    low = jnp.where(even, first, roll(second, HALF))
    high = jnp.where(even, roll(first, -HALF), second)
    return low, high


def complex_dot(table, tiles, sign):
    real = jnp.concatenate(tiles, axis=1)
    turned = jnp.concatenate([rotated(tile, sign) for tile in tiles], axis=1)
    return table_dot(table, jnp.concatenate([real, turned], axis=0))


def z_forward_kernel(volume, table, out, field, held, sems):
    copies = []
    for part in range(4):
        place = pl.ds(part * 8, 8)
        copies.append(pltpu.make_async_copy(volume.at[place], field.at[place], sems.at[part]))
    for part in range(4):
        place = pl.ds(part * 128, 128)
        copies.append(pltpu.make_async_copy(table.at[place], held.at[place], sems.at[4 + part]))
    for copy in copies:
        copy.start()
    for copy in copies[:4]:
        copy.wait()
    high, low = split(jnp.concatenate([field[:, y, :] for y in range(8)], axis=0))
    for copy in copies[4:]:
        copy.wait()
    res = dot(jnp.concatenate([high, low], axis=0), held[:M])
    res = res[:M] + (res[M:] + dot(high, held[M:]))
    for pair in range(GX // 2):
        tile = res[:, pair * 128 : pair * 128 + 128]
        first, second = exchange(tile[:128], tile[128:])
        out[2 * pair, :128] = first
        out[2 * pair + 1, :128] = second
    edge = res[:, GX * 64 :]
    lane = lax.broadcasted_iota(jnp.int32, (32, 128), 1)
    planes = jnp.zeros((32, 128), jnp.float32)
    for y in range(8):
        planes = jnp.where(lane % 8 == y, edge[y * 32 : y * 32 + 32], planes)
    lane = lax.broadcasted_iota(jnp.int32, (8, 128), 1)
    for block in range(GX):
        tile = jnp.zeros((8, 128), jnp.float32)
        for quarter in range(4):
            moved = roll(planes[quarter * 8 : quarter * 8 + 8], 16 * quarter - 16 * block)
            tile = jnp.where(lane // 16 == quarter, moved, tile)
        out[block, 128:] = tile


def x_forward_kernel(received, held, table, out):
    for pair in range(2):
        tiles = [
            received[:, y * 32 : y * 32 + 32, :].reshape(M, 128) for y in (2 * pair, 2 * pair + 1)
        ]
        res = complex_dot(table, tiles, 1.0)
        for at in range(2):
            blocks = res[:, at * 128 : at * 128 + 128].reshape(GA, 2, 8, 128)
            first, second = exchange(blocks[:, 0].reshape(M, 128), blocks[:, 1].reshape(M, 128))
            out[:, 2 * pair + at] = first.reshape(GA, 8, 128)
            out[:, 2 * pair + at + 4] = second.reshape(GA, 8, 128)
    lane = lax.broadcasted_iota(jnp.int32, (8, 128), 1)
    rows = []
    for block in range(GX):
        tile = received[block, 128:, :]
        for quarter in range(4):
            real = roll(tile, -16 * quarter)
            imag = roll(tile, 56 - 16 * quarter)
            rows.append(jnp.where(lane < 64, real, imag))
    res = complex_dot(table, [jnp.concatenate(rows, axis=0)], 1.0).T
    for group in range(GA):
        cols = slice(group // 8 * 128, group // 8 * 128 + 128)
        shift = -16 * (group % 8)
        out[group, 8] = jnp.where(
            lane < 64, roll(res[0:8, cols], shift), roll(res[64:72, cols], shift + 64)
        )


def doubled(tile):
    first, second = tile[:, :64], tile[:, 64:]
    return jnp.concatenate([first, first, second, second], axis=1)


def pair_order(pair):
    return 2 * pair, 2 * pair + 8, 2 * pair + 1, 2 * pair + 9


def flipped(rows):
    shape = (128, 128)
    at, source = (lax.broadcasted_iota(jnp.int32, shape, axis) for axis in (0, 1))
    planes = (at // HALF == source // HALF) & (at % HALF + source % HALF == HALF)
    planes = jnp.where(planes, 1.0, 0.0).astype(BF)
    at, source = (lax.broadcasted_iota(jnp.int32, (N, N), axis) for axis in (0, 1))
    flip = jnp.where((at + source) % N == 0, 1.0, 0.0).astype(BF)
    count = rows.shape[0]
    high, low = [], []
    for first in range(0, count, 128):
        block = dot(planes, jnp.concatenate(split(rows[first : first + 128]), axis=1))
        upper, lower = split(block[:, :N] + block[:, N:])
        high.append(upper)
        low.append(lower)
    res = dot(jnp.concatenate(high + low, axis=0), flip)
    return res[:count] + res[count:]


def turn_kernel(own, late, early, rows, sems):
    copies = [
        pltpu.make_async_copy(own.at[k, pl.ds(HALF, HALF)], rows.at[k], sems.at[k])
        for k in range(16)
    ]
    for copy in copies:
        copy.start()
    for copy in copies:
        copy.wait()
    res = flipped(jnp.concatenate([rows[(16 - k) % 16] for k in range(1, 17)], axis=0))
    res = res.reshape(16, HALF, N)
    early[:EARLY] = res[:EARLY]
    early[EARLY:] = res[15:]
    late[...] = res[EARLY:15]


def own_kernel(own, volume, prior, out, partial):
    field = volume[...]
    partial[...] = fold((prior[...] * field * field).reshape(M, M))
    for pair in range(4):
        rows = jnp.concatenate([own[k, :HALF] for k in pair_order(pair)], axis=0)
        out[:, pair * 256 : pair * 256 + 256] = doubled(rows.T)
    edge = jnp.concatenate([own[:, HALF, :], jnp.zeros((48, N), jnp.float32)] * 2, axis=0)
    out[:, 1024:] = edge.T


def y_forward_kernel(received, table, out):
    for pair in range(4):
        tiles = []
        for at in range(2):
            rows = [
                received[pl.ds(group * 72 + pair * 2 + at, 8, stride=8), :] for group in range(GA)
            ]
            tiles.append(jnp.concatenate(rows, axis=0))
        out[:, pair * 256 : pair * 256 + 256] = complex_dot(table, tiles, 1.0)
    rows = [received[group * 72 + 64 : group * 72 + 72, :] for group in range(GA)]
    out[:, 1024:] = complex_dot(table, [jnp.concatenate(rows, axis=0)], 1.0)


def y_inverse_kernel(spectrum, base, far, near, rim, partial, table, out):
    def extra(pair):
        rows = [
            far[k - EARLY - 1] if k > EARLY else near[k - 1] if k else rim[0]
            for k in pair_order(pair)
        ]
        return doubled(jnp.concatenate(rows, axis=0).T)

    total = partial[...]
    for pair in range(5):
        place = slice(pair * 256, min(pair * 256 + 256, 1152))
        scale = base[:, place]
        if pair < 4:
            scale += extra(pair)
        values = spectrum[:, place]
        weighted = values * scale
        total += fold(weighted * values) * (1.0 / float(N) ** 3)
        cols = [weighted[:, at : at + 128] for at in range(0, values.shape[1], 128)]
        res = complex_dot(table, cols, -1.0)
        if pair == 4:
            res = jnp.where(lanes(res) < 96, res, jnp.sum(total))
        out[:, :, place] = res.reshape(GA, 8, res.shape[1])


def x_inverse_kernel(received, table, plain, out):
    for pair in range(2):
        tiles = []
        for y in (2 * pair, 2 * pair + 1):
            first, second = (
                jnp.concatenate(
                    [received[:, at, k * 128 : k * 128 + 128] for k in range(8)], axis=0
                )
                for at in (y, y + 4)
            )
            tiles.append(jnp.concatenate(exchange(first, second), axis=0))
        res = complex_dot(table, tiles, -1.0)
        for at in range(2):
            y = 2 * pair + at
            out[:, y * 32 : y * 32 + 32, :] = res[:, at * 128 : at * 128 + 128].reshape(GX, 32, 128)
    lane = lax.broadcasted_iota(jnp.int32, (8, 128), 1)
    real, imag = [], []
    count = jnp.zeros((1, 1), jnp.float32)
    for four in range(4):
        real_tile = jnp.zeros((8, 128), jnp.float32)
        imag_tile = real_tile
        for at in range(8):
            tile = received[four * 8 + at, :, 1024:]
            count += tile[:1, 127:]
            here = lane // 16 == at
            real_tile = jnp.where(here, roll(tile, 16 * at), real_tile)
            imag_tile = jnp.where(here, roll(tile, 16 * at - 64), imag_tile)
        real.append(real_tile)
        imag.append(imag_tile)
    blank = jnp.zeros((56, N), jnp.float32)
    stacked = jnp.concatenate(
        [jnp.concatenate(real, axis=1), blank, jnp.concatenate(imag, axis=1), blank], axis=0
    )
    res = complex_dot(plain, [stacked.T], -1.0)
    for block in range(GX):
        tile = jnp.broadcast_to(count, (8, 128))
        for quarter in range(4):
            part = res[block * 32 + quarter * 8 : block * 32 + quarter * 8 + 8]
            tile = jnp.where(lane // 8 == 2 * quarter, roll(part, 16 * quarter), tile)
            tile = jnp.where(lane // 8 == 2 * quarter + 1, roll(part, 16 * quarter - 56), tile)
        out[block, 128:] = tile


def z_inverse_kernel(received, volume, prior, table, out, curvature):
    lower, upper = [], []
    for pair in range(GX // 2):
        first, second = exchange(received[2 * pair, :128], received[2 * pair + 1, :128])
        lower.append(first)
        upper.append(second)
    lane = lax.broadcasted_iota(jnp.int32, (8, 128), 1)
    planes = []
    for quarter in range(4):
        tile = jnp.zeros((8, 128), jnp.float32)
        for block in range(GX):
            moved = roll(received[block, 128:], 16 * block - 16 * quarter)
            tile = jnp.where(lane // 16 == block, moved, tile)
        planes.append(tile)
    planes = jnp.concatenate(planes, axis=0)
    edge = jnp.concatenate(
        [jnp.where(lanes(planes) % 8 == y, planes, 0.0) for y in range(8)], axis=0
    )
    main = jnp.concatenate(
        [jnp.concatenate(lower, axis=1), jnp.concatenate(upper, axis=1)], axis=0
    )
    image = data_dot(jnp.concatenate([main, edge], axis=1), table)
    for y in range(8):
        out[:, y, :] = image[y * 32 : y * 32 + 32, :] + prior[:, y, :] * volume[:, y, :]
    total = jnp.sum(received[:, 128:, 127:].reshape(GX * 8, 1)) / 8.0
    curvature[0] = total / float(M) ** 3


def whole():
    return pl.BlockSpec(memory_space=pltpu.VMEM)


def anywhere():
    return pl.BlockSpec(memory_space=pl.ANY)


def in_hbm():
    return pl.BlockSpec(memory_space=pltpu.HBM)


def params(limit=VM):
    return pltpu.CompilerParams(vmem_limit_bytes=limit * 1024 * 1024)


def cost(micros):
    return pl.CostEstimate(flops=int(micros * 1e9), bytes_accessed=8 << 20, transcendentals=0)


def f32(*shape):
    return jax.ShapeDtypeStruct(shape, jnp.float32)


def mirror(value):
    pairs = [(GA - 1 - group, group) for group in range(GA)]
    return lax.ppermute(value, ("gy", "gz"), pairs)


def onward(value):
    return lax.ppermute(value, ("gy", "gz"), [(group, (group + 1) % GA) for group in range(GA)])


def reflect(value):
    count = GX * GA
    return lax.ppermute(value, AXES, [(count - 1 - at, at) for at in range(count)])


def opposite(value):
    return lax.ppermute(value, "gx", [(GX - 1 - block, block) for block in range(GX)])


def local(volume, prior_weight, kernel):
    late, early = pl.pallas_call(
        turn_kernel,
        out_shape=(f32(LATE, HALF, N), f32(EARLY + 1, HALF, N)),
        in_specs=[in_hbm()],
        out_specs=(whole(), whole()),
        scratch_shapes=[pltpu.VMEM((16, HALF, N), jnp.float32), pltpu.SemaphoreType.DMA((16,))],
        compiler_params=params(63),
        cost_estimate=cost(TURN_COST),
        name="turn",
    )(kernel)
    plane = mirror(late)
    near = reflect(early)
    rim = onward(near[EARLY:])
    base, partial = pl.pallas_call(
        own_kernel,
        out_shape=(f32(N, 1152), f32(8, 128)),
        in_specs=[whole()] * 3,
        out_specs=(whole(), whole()),
        compiler_params=params(),
        cost_estimate=cost(OWN_COST),
        name="own_weights",
    )(kernel, volume, prior_weight)
    sent = pl.pallas_call(
        z_forward_kernel,
        out_shape=f32(GX, 136, 128),
        in_specs=[in_hbm()] * 2,
        out_specs=whole(),
        scratch_shapes=[
            pltpu.VMEM((32, 8, M), jnp.float32),
            pltpu.VMEM((2 * M, 640), BF),
            pltpu.SemaphoreType.DMA((8,)),
        ],
        compiler_params=params(63),
        name="z_forward",
    )(volume, z_forward_table())
    got = lax.all_to_all(sent, "gx", split_axis=0, concat_axis=0, tiled=True)
    far = opposite(plane)
    sent = pl.pallas_call(
        x_forward_kernel,
        out_shape=f32(GA, 9, 8, 128),
        in_specs=[whole(), anywhere(), whole()],
        out_specs=whole(),
        compiler_params=params(),
        name="x_forward",
    )(got, plane, forward_table())
    got = lax.all_to_all(sent, ("gy", "gz"), split_axis=0, concat_axis=0, tiled=True)
    spectrum = pl.pallas_call(
        y_forward_kernel,
        out_shape=f32(N, 1152),
        in_specs=[whole()] * 2,
        out_specs=whole(),
        compiler_params=params(),
        cost_estimate=cost(FORWARD_COST),
        name="y_forward",
    )(got.reshape(GA * 72, 128), forward_table())
    sent = pl.pallas_call(
        y_inverse_kernel,
        out_shape=f32(GA, 8, 1152),
        in_specs=[whole()] * 7,
        out_specs=whole(),
        compiler_params=params(),
        name="y_inverse",
    )(spectrum, base, far, near, rim, partial, inverse_table())
    got = lax.all_to_all(sent, ("gy", "gz"), split_axis=0, concat_axis=0, tiled=True)
    sent = pl.pallas_call(
        x_inverse_kernel,
        out_shape=f32(GX, 136, 128),
        in_specs=[whole()] * 3,
        out_specs=whole(),
        compiler_params=params(),
        name="x_inverse",
    )(got, x_inverse_table(), inverse_table())
    got = lax.all_to_all(sent, "gx", split_axis=0, concat_axis=0, tiled=True)
    product, curvature = pl.pallas_call(
        z_inverse_kernel,
        out_shape=(f32(32, 8, M), f32(1)),
        in_specs=[whole()] * 4,
        out_specs=(whole(), pl.BlockSpec(memory_space=pltpu.SMEM)),
        compiler_params=params(),
        name="z_inverse",
    )(got, volume, prior_weight, z_inverse_table())
    return product, curvature


def solution(mesh):
    return jax.shard_map(
        local,
        mesh=mesh,
        in_specs=(
            P("gx", ("gy", "gz"), None),
            P("gx", ("gy", "gz"), None),
            P(("gy", "gz"), "gx", None),
        ),
        out_specs=(P("gx", ("gy", "gz"), None), P()),
        check_vma=False,
    )
```

time: 140 us -> 135 us (0.964)
  blocking collectives: 45.7 us -> 51.6 us
  starting transfers between devices: 37 us -> 32.5 us
  Pallas kernels: 23.6 us -> 19.3 us
  local copies, waits for them, and re-layouts: 11.5 us -> 7.44 us
  waiting for transfers between devices: 20.3 us -> 22.4 us
    ppermute x3 -> x1, starting transfers between devices: 12.2 us -> 1.71 us  [opposite(): lax.ppermute(value, 'gx', [(GX - 1 - block, block) for block in range(GX)])]
    ppermute x3 -> x1, starting transfers between devices: 13.9 us -> 5.86 us  [mirror(): return lax.ppermute(value, ('gy', 'gz'), pairs)]
    ppermute x3 -> x1, waiting for transfers between devices: 6.35 us -> 12.2 us  [mirror(): return lax.ppermute(value, ('gy', 'gz'), pairs)]
    ppermute x0 -> x2, starting transfers between devices: none -> 5.65 us  [the longest x1 2.89 us: onward(): lax.ppermute(value, ('gy', 'gz'), [(group, (group + 1) % GA) for group in...]
    all_to_all x1, starting transfers between devices: 3.54 us -> 9.03 us  [local(): got = lax.all_to_all(sent, 'gx', split_axis=0, concat_axis=0, tiled=True)]
    unnamed x44 -> x20, local copies, waits for them, and re-layouts: 10.4 us -> 5.96 us
    all_to_all x1, waiting for transfers between devices: 13.9 us -> 10.1 us  [local(): lax.all_to_all(sent, ('gy', 'gz'), split_axis=0, concat_axis=0, tiled=True)]
    all_to_all x1, blocking collectives: 23 us -> 26.6 us  [local(): got = lax.all_to_all(sent, 'gx', split_axis=0, concat_axis=0, tiled=True)]
  transfers between devices with their start and end apart: 8 -> 6, of which waited for: 2 -> 2; matrix products, arithmetic and copies ran while one was open for 0% -> 1% of each run, Pallas kernels for 10% -> 7%
where the time goes in v2:
time: 135 us; the launch traced here: 134 us
  blocking collectives  51.6 us (38%)
  starting transfers between devices  32.5 us (24%)
  waiting for transfers between devices  22.4 us (17%)
  Pallas kernels  19.3 us (14%)
  local copies, waits for them, and re-layouts  7.44 us (6%)
    all_to_all x1, blocking collectives, local(): got = lax.all_to_all(sent, 'gx', split_axis=0, concat_axis=0, tiled=True)  26.6 us
    all_to_all x1, blocking collectives, local(): lax.all_to_all(sent, ('gy', 'gz'), split_axis=0, concat_axis=0, tiled=True)  25.1 us
    ppermute x1, waiting for transfers between devices, mirror(): return lax.ppermute(value, ('gy', 'gz'), pairs)  12.2 us
    all_to_all x1, starting transfers between devices, local(): lax.all_to_all(sent, ('gy', 'gz'), split_axis=0, concat_axis=0, tiled=True)  10.3 us
    all_to_all x1, waiting for transfers between devices, local(): lax.all_to_all(sent, ('gy', 'gz'), split_axis=0, concat_axis=0, tiled=True)  10.1 us
    all_to_all x1, starting transfers between devices, local(): got = lax.all_to_all(sent, 'gx', split_axis=0, concat_axis=0, tiled=True)  9.03 us
    unnamed x20, local copies, waits for them, and re-layouts  5.96 us
    ppermute x1, starting transfers between devices, mirror(): return lax.ppermute(value, ('gy', 'gz'), pairs)  5.86 us
  transfers between devices with their start and end apart: 6, of which 2 were waited for; matrix products, arithmetic and copies ran while one was open for 1% of the time, Pallas kernels for 7%

profile of v2, /device:TPU:1, one launch (start us, length us, event | category | flops | bytes accessed | tf_op | source)
XLA Modules:
  0.0 134.2 jit_solution(2661518430407468588)
XLA Ops:
  0.6 2.7 %z_forward.1 = f32[8,136,128]{2,1,0:T(8,128)} custom-call(f32[32,8,256]{2,1,0:T(8,128)} %volume.5, bf16[512,640]{1,0:T(8,128)(2,1)} %constant.10.clone.table), custom_call_target="tpu_custom_call" | custom-call | tf_op jit(solution)/shard_map/z_forward/pallas_call | solution.py:427
  3.4 9.0 %all-to-all-start = ((f32[8,136,128]{2,1,0:T(8,128)}), f32[8,136,128]{2,1,0:T(8,128)S(1)}, u32[]{:S(2)}, u32[]{:S(2)}) async-start(f32[8,136,128]{2,1,0:T(8,128)} %z_forward.1), calls=%async_computation | async-start | bytes 1114112 | tf_op jit(solution)/shard_map/all_to_all | solution.py:440
  12.4 3.3 %turn.1 = (f32[9,32,512]{2,1,0:T(8,128)}, f32[7,32,512]{2,1,0:T(8,128)}) custom-call(f32[16,64,512]{2,1,0:T(8,128)} %own.3), custom_call_target="tpu_custom_call" | custom-call | flops 8000000000 | bytes 8388608 | tf_op jit(solution)/shard_map/turn/pallas_call | solution.py:405
  15.7 5.9 %collective-permute-start = (f32[9,32,512]{2,1,0:T(8,128)}, f32[9,32,512]{2,1,0:T(8,128)}, u32[]{:S(2)}, u32[]{:S(2)}) collective-permute-start(f32[9,32,512]{2,1,0:T(8,128)} %get-tuple-element.6), channel_id=1, source_target_pairs={{31,0},{30,1},{29,2},{28,3},{27,4},{26,5},{25,6},{24,7},{23,8},{22... | collective-permute-start | bytes 1769480 | tf_op jit(solution)/shard_map/ppermute | solution.py:388
  21.6 2.8 %collective-permute-start.2 = (f32[7,32,512]{2,1,0:T(8,128)}, f32[7,32,512]{2,1,0:T(8,128)}, u32[]{:S(2)}, u32[]{:S(2)}) collective-permute-start(f32[7,32,512]{2,1,0:T(8,128)} %get-tuple-element.8), channel_id=1, source_target_pairs={{255,0},{254,1},{253,2},{252,3},{251,4},{250,5},{249,6},{248,7},{2... | collective-permute-start | bytes 1376264 | tf_op jit(solution)/shard_map/ppermute | solution.py:397
  24.3 12.2 %collective-permute-done.held = f32[9,32,512]{2,1,0:T(8,128)} collective-permute-done((f32[9,32,512]{2,1,0:T(8,128)}, f32[9,32,512]{2,1,0:T(8,128)}, u32[]{:S(2)}, u32[]{:S(2)}) %collective-permute-start) | collective-permute-done | bytes 589856 | tf_op jit(solution)/shard_map/ppermute | solution.py:388
  36.6 1.7 %collective-permute-start.1 = (f32[9,32,512]{2,1,0:T(8,128)}, f32[9,32,512]{2,1,0:T(8,128)}, u32[]{:S(2)}, u32[]{:S(2)}) collective-permute-start(f32[9,32,512]{2,1,0:T(8,128)} %collective-permute-done.held), channel_id=1, source_target_pairs={{224,0},{192,32},{160,64},{128,96},{96,128},{64,160},{32,192},{0,2... | collective-permute-start | bytes 1769480 | tf_op jit(solution)/shard_map/ppermute | solution.py:401
  38.3 0.0 all-to-all-done.received
  38.3 1.2 copy-done.1
  39.5 2.7 %x_forward.1 = f32[32,9,8,128]{3,2,1,0:T(8,128)} custom-call(f32[8,136,128]{2,1,0:T(8,128)S(1)} %all-to-all-done.received, f32[9,32,512]{2,1,0:T(8,128)} %collective-permute-done.held, bf16[512,1024]{1,0:T(8,128)(2,1)S(1)} %copy-done.1), custom_call_target="tpu_custom_call" | custom-call | tf_op jit(solution)/shard_map/x_forward/pallas_call | solution.py:442
  42.2 10.3 %all-to-all-start.1 = ((f32[32,9,8,128]{3,2,1,0:T(8,128)}), f32[32,9,8,128]{3,2,1,0:T(8,128)S(1)}, u32[]{:S(2)}, u32[]{:S(2)}) async-start(f32[32,9,8,128]{3,2,1,0:T(8,128)} %x_forward.1), calls=%async_computation.1 | async-start | bytes 2359296 | tf_op jit(solution)/shard_map/all_to_all | solution.py:450
  52.5 0.0 copy-start.4
  52.5 0.9 copy-done.4
  53.5 0.9 copy-done.7
  54.4 1.6 %copy-done.9 = f32[16,64,512]{2,1,0:T(8,128)S(1)} copy-done((f32[16,64,512]{2,1,0:T(8,128)S(1)}, f32[16,64,512]{2,1,0:T(8,128)}, u32[]{:S(2)}) %copy-start.9) | copy-done | bytes 2097176
  56.0 0.7 own_weights.1
  56.7 0.0 collective-permute-done.2.near
  56.7 1.5 %slice.4 = f32[1,32,512]{2,1,0:T(8,128)} slice(f32[7,32,512]{2,1,0:T(8,128)} %collective-permute-done.2.near), slice={[6:7], [0:32], [0:512]} | slice | bytes 131072 | tf_op jit(solution)/shard_map/slice | solution.py:417
  58.2 2.9 %collective-permute-start.3 = (f32[1,32,512]{2,1,0:T(8,128)}, f32[1,32,512]{2,1,0:T(8,128)}, u32[]{:S(2)}, u32[]{:S(2)}) collective-permute-start(f32[1,32,512]{2,1,0:T(8,128)} %slice.4), channel_id=1, source_target_pairs={{0,1},{1,2},{2,3},{3,4},{4,5},{5,6},{6,7},{7,8},{8,9},{9,10},{10,1... | collective-permute-start | bytes 196616 | tf_op jit(solution)/shard_map/ppermute | solution.py:392
  61.1 10.1 %all-to-all-done.1 = f32[32,9,8,128]{3,2,1,0:T(8,128)S(1)} async-done(((f32[32,9,8,128]{3,2,1,0:T(8,128)}), f32[32,9,8,128]{3,2,1,0:T(8,128)S(1)}, u32[]{:S(2)}, u32[]{:S(2)}) %all-to-all-start.1) | async-done | bytes 1179680 | tf_op jit(solution)/shard_map/all_to_all | solution.py:450
  71.2 1.2 copy-done.2
  72.5 2.3 %y_forward.1.spectrum = f32[512,1152]{1,0:T(8,128)S(1)} custom-call(f32[2304,128]{1,0:T(8,128)S(1)} %bitcast.1, bf16[512,1024]{1,0:T(8,128)(2,1)S(1)} %copy-done.2), custom_call_target="tpu_custom_call" | custom-call | flops 5000000000 | bytes 8388608 | tf_op jit(solution)/shard_map/y_forward/pallas_call | solution.py:451
  74.8 0.0 collective-permute-done.3.rim
  74.8 0.0 collective-permute-done.1.far
  74.8 4.1 %y_inverse.1 = f32[32,8,1152]{2,1,0:T(8,128)S(1)} custom-call(f32[512,1152]{1,0:T(8,128)S(1)} %y_forward.1.spectrum, f32[512,1152]{1,0:T(8,128)S(1)} %get-tuple-element.7.base, f32[9,32,512]{2,1,0:T(8,128)} %collective-permute-done.1.far, f32[7,32,512]{2,1,0:T(8,128)} %collective-permute-done.2.near, f32[1,32,512]{2,1,0:T(8,128)} %collective-permute-done.3.rim, ...), custom_call_target="tpu_custom_call" | custom-call | tf_op jit(solution)/shard_map/y_inverse/pallas_call | solution.py:460
  78.9 0.0 copy-start.3
  78.9 25.1 %all_to_all.20.received = f32[32,8,1152]{2,1,0:T(8,128)S(1)} all-to-all(f32[32,8,1152]{2,1,0:T(8,128)S(1)} %y_inverse.1), channel_id=1, replica_groups=mesh['gx'=8,'gy'=4,'gz'=8] {'gy','gz'}, dimensions={0} | all-to-all | bytes 2359296 | tf_op jit(solution)/shard_map/all_to_all | solution.py:468
  103.9 2.1 %x_inverse.1 = f32[8,136,128]{2,1,0:T(8,128)S(1)} custom-call(f32[32,8,1152]{2,1,0:T(8,128)S(1)} %all_to_all.20.received, bf16[256,2048]{1,0:T(8,128)(2,1)S(1)} %copy-done.3, bf16[256,2048]{1,0:T(8,128)(2,1)S(1)} %copy-done), custom_call_target="tpu_custom_call" | custom-call | tf_op jit(solution)/shard_map/x_inverse/pallas_call | solution.py:469
  106.1 0.0 copy-start.5
  106.1 0.0 copy-start.8
  106.1 26.6 %all_to_all.21.received = f32[8,136,128]{2,1,0:T(8,128)S(1)} all-to-all(f32[8,136,128]{2,1,0:T(8,128)S(1)} %x_inverse.1), channel_id=1, replica_groups=mesh['gx'=8,'gy'=4,'gz'=8] {'gx'}, dimensions={0} | all-to-all | bytes 1114112 | tf_op jit(solution)/shard_map/all_to_all | solution.py:477
  132.7 1.3 %z_inverse.1 = (f32[32,8,256]{2,1,0:T(8,128)}, f32[1]{0:T(128)}) custom-call(f32[8,136,128]{2,1,0:T(8,128)S(1)} %all_to_all.21.received, f32[32,8,256]{2,1,0:T(8,128)S(1)} %copy-done.5, f32[32,8,256]{2,1,0:T(8,128)S(1)} %copy-done.8, bf16[1920,256]{1,0:T(8,128)(2,1)S(1)} %copy-done.6), custom_call_target="tpu_custom_call" | custom-call | tf_op jit(solution)/shard_map/z_inverse/pallas_call | solution.py:478
  (11 shorter events, 0.0 us)
Async XLA Ops:
  3.4 34.9 %all-to-all-start = ((f32[8,136,128]{2,1,0:T(8,128)}), f32[8,136,128]{2,1,0:T(8,128)S(1)}, u32[]{:S(2)}, u32[]{:S(2)}) async-start(f32[8,136,128]{2,1,0:T(8,128)} %z_forward.1), calls=%async_computation | async-start | bytes 1114112 | tf_op jit(solution)/shard_map/all_to_all | solution.py:440
  15.7 20.9 %collective-permute-start = (f32[9,32,512]{2,1,0:T(8,128)}, f32[9,32,512]{2,1,0:T(8,128)}, u32[]{:S(2)}, u32[]{:S(2)}) collective-permute-start(f32[9,32,512]{2,1,0:T(8,128)} %get-tuple-element.6), channel_id=1, source_target_pairs={{31,0},{30,1},{29,2},{28,3},{27,4},{26,5},{25,6},{24,7},{23,8},{22... | collective-permute-start | bytes 1769480 | tf_op jit(solution)/shard_map/ppermute | solution.py:388
  21.6 35.2 %collective-permute-start.2 = (f32[7,32,512]{2,1,0:T(8,128)}, f32[7,32,512]{2,1,0:T(8,128)}, u32[]{:S(2)}, u32[]{:S(2)}) collective-permute-start(f32[7,32,512]{2,1,0:T(8,128)} %get-tuple-element.8), channel_id=1, source_target_pairs={{255,0},{254,1},{253,2},{252,3},{251,4},{250,5},{249,6},{248,7},{2... | collective-permute-start | bytes 1376264 | tf_op jit(solution)/shard_map/ppermute | solution.py:397
  36.6 38.2 %collective-permute-start.1 = (f32[9,32,512]{2,1,0:T(8,128)}, f32[9,32,512]{2,1,0:T(8,128)}, u32[]{:S(2)}, u32[]{:S(2)}) collective-permute-start(f32[9,32,512]{2,1,0:T(8,128)} %collective-permute-done.held), channel_id=1, source_target_pairs={{224,0},{192,32},{160,64},{128,96},{96,128},{64,160},{32,192},{0,2... | collective-permute-start | bytes 1769480 | tf_op jit(solution)/shard_map/ppermute | solution.py:401
  38.3 1.2 copy-start.1
  42.2 29.0 %all-to-all-start.1 = ((f32[32,9,8,128]{3,2,1,0:T(8,128)}), f32[32,9,8,128]{3,2,1,0:T(8,128)S(1)}, u32[]{:S(2)}, u32[]{:S(2)}) async-start(f32[32,9,8,128]{3,2,1,0:T(8,128)} %x_forward.1), calls=%async_computation.1 | async-start | bytes 2359296 | tf_op jit(solution)/shard_map/all_to_all | solution.py:450
  52.5 1.0 copy-start.4
  53.5 0.9 copy-start.7
  54.4 1.6 %copy-start.9 = (f32[16,64,512]{2,1,0:T(8,128)S(1)}, f32[16,64,512]{2,1,0:T(8,128)}, u32[]{:S(2)}) copy-start(f32[16,64,512]{2,1,0:T(8,128)} %own.3) | copy-start | bytes 6291460
  58.2 16.6 %collective-permute-start.3 = (f32[1,32,512]{2,1,0:T(8,128)}, f32[1,32,512]{2,1,0:T(8,128)}, u32[]{:S(2)}, u32[]{:S(2)}) collective-permute-start(f32[1,32,512]{2,1,0:T(8,128)} %slice.4), channel_id=1, source_target_pairs={{0,1},{1,2},{2,3},{3,4},{4,5},{5,6},{6,7},{7,8},{8,9},{9,10},{10,1... | collective-permute-start | bytes 196616 | tf_op jit(solution)/shard_map/ppermute | solution.py:392
  71.2 1.2 copy-start.2
  72.5 2.3 %copy-start = (bf16[256,2048]{1,0:T(8,128)(2,1)S(1)}, bf16[256,2048]{1,0:T(8,128)(2,1)}, u32[]{:S(2)}) copy-start(bf16[256,2048]{1,0:T(8,128)(2,1)} %constant.12.clone.table.plain) | copy-start | bytes 3145732
  78.9 25.1 %copy-start.3 = (bf16[256,2048]{1,0:T(8,128)(2,1)S(1)}, bf16[256,2048]{1,0:T(8,128)(2,1)}, u32[]{:S(2)}) copy-start(bf16[256,2048]{1,0:T(8,128)(2,1)} %constant.13.clone.table) | copy-start | bytes 3145732
  103.9 28.7 %copy-start.6 = (bf16[1920,256]{1,0:T(8,128)(2,1)S(1)}, bf16[1920,256]{1,0:T(8,128)(2,1)}, u32[]{:S(2)}) copy-start(bf16[1920,256]{1,0:T(8,128)(2,1)} %constant.14.clone.table) | copy-start | bytes 2949124
  106.1 26.6 %copy-start.5 = (f32[32,8,256]{2,1,0:T(8,128)S(1)}, f32[32,8,256]{2,1,0:T(8,128)}, u32[]{:S(2)}) copy-start(f32[32,8,256]{2,1,0:T(8,128)} %volume.5) | copy-start | bytes 786436
  106.1 26.6 %copy-start.8 = (f32[32,8,256]{2,1,0:T(8,128)S(1)}, f32[32,8,256]{2,1,0:T(8,128)}, u32[]{:S(2)}) copy-start(f32[32,8,256]{2,1,0:T(8,128)} %prior.3) | copy-start | bytes 786436

commit v3 on v2

--- a/solution.py
+++ b/solution.py
@@ -80,7 +80,7 @@
 
 
 def stack_left(table):
-    return np.concatenate(halves(table), axis=1)
+    return np.concatenate(halves(table), axis=0)
 
 
 def stack_right(table):
@@ -90,8 +90,9 @@
 
 def table_dot(table, data):
     high, low = split(data)
-    depth = data.shape[0]
-    return dot(table[...], jnp.concatenate([high, high], axis=0)) + dot(table[:, :depth], low)
+    count = table.shape[0] // 2
+    wide = dot(table[...], high)
+    return wide[:count] + (wide[count:] + dot(table[:count], low))
 
 
 def data_dot(data, table):

time: 135 us -> 134 us (level)
  no operation moved by 1% of the time
where the time goes in v3:
time: 134 us
  blocking collectives  51.6 us (39%)
  starting transfers between devices  32.5 us (24%)
  waiting for transfers between devices  22.4 us (17%)
  Pallas kernels  18.7 us (14%)
  local copies, waits for them, and re-layouts  7.44 us (6%)
    all_to_all x1, blocking collectives, local(): got = lax.all_to_all(sent, 'gx', split_axis=0, concat_axis=0, tiled=True)  26.6 us
    all_to_all x1, blocking collectives, local(): lax.all_to_all(sent, ('gy', 'gz'), split_axis=0, concat_axis=0, tiled=True)  25 us
    ppermute x1, waiting for transfers between devices, mirror(): return lax.ppermute(value, ('gy', 'gz'), pairs)  12.2 us
    all_to_all x1, starting transfers between devices, local(): lax.all_to_all(sent, ('gy', 'gz'), split_axis=0, concat_axis=0, tiled=True)  10.3 us
    all_to_all x1, waiting for transfers between devices, local(): lax.all_to_all(sent, ('gy', 'gz'), split_axis=0, concat_axis=0, tiled=True)  10.1 us
    all_to_all x1, starting transfers between devices, local(): got = lax.all_to_all(sent, 'gx', split_axis=0, concat_axis=0, tiled=True)  9.03 us
    unnamed x20, local copies, waits for them, and re-layouts  5.96 us
    ppermute x1, starting transfers between devices, mirror(): return lax.ppermute(value, ('gy', 'gz'), pairs)  5.86 us
  transfers between devices with their start and end apart: 6, of which 2 were waited for; matrix products, arithmetic and copies ran while one was open for 1% of the time, Pallas kernels for 7%

profile of v3, /device:TPU:1, one launch (start us, length us, event | category | flops | bytes accessed | tf_op | source)
XLA Modules:
  0.0 133.6 jit_solution(7696288952998610618)
XLA Ops:
  0.6 2.7 %z_forward.1 = f32[8,136,128]{2,1,0:T(8,128)} custom-call(f32[32,8,256]{2,1,0:T(8,128)} %volume.5, bf16[512,640]{1,0:T(8,128)(2,1)} %constant.10.clone.table), custom_call_target="tpu_custom_call" | custom-call | tf_op jit(solution)/shard_map/z_forward/pallas_call | solution.py:428
  3.4 9.0 %all-to-all-start = ((f32[8,136,128]{2,1,0:T(8,128)}), f32[8,136,128]{2,1,0:T(8,128)S(1)}, u32[]{:S(2)}, u32[]{:S(2)}) async-start(f32[8,136,128]{2,1,0:T(8,128)} %z_forward.1), calls=%async_computation | async-start | bytes 1114112 | tf_op jit(solution)/shard_map/all_to_all | solution.py:441
  12.4 3.3 %turn.1 = (f32[9,32,512]{2,1,0:T(8,128)}, f32[7,32,512]{2,1,0:T(8,128)}) custom-call(f32[16,64,512]{2,1,0:T(8,128)} %own.3), custom_call_target="tpu_custom_call" | custom-call | flops 8000000000 | bytes 8388608 | tf_op jit(solution)/shard_map/turn/pallas_call | solution.py:406
  15.7 5.9 %collective-permute-start = (f32[9,32,512]{2,1,0:T(8,128)}, f32[9,32,512]{2,1,0:T(8,128)}, u32[]{:S(2)}, u32[]{:S(2)}) collective-permute-start(f32[9,32,512]{2,1,0:T(8,128)} %get-tuple-element.6), channel_id=1, source_target_pairs={{31,0},{30,1},{29,2},{28,3},{27,4},{26,5},{25,6},{24,7},{23,8},{22... | collective-permute-start | bytes 1769480 | tf_op jit(solution)/shard_map/ppermute | solution.py:389
  21.6 2.8 %collective-permute-start.2 = (f32[7,32,512]{2,1,0:T(8,128)}, f32[7,32,512]{2,1,0:T(8,128)}, u32[]{:S(2)}, u32[]{:S(2)}) collective-permute-start(f32[7,32,512]{2,1,0:T(8,128)} %get-tuple-element.8), channel_id=1, source_target_pairs={{255,0},{254,1},{253,2},{252,3},{251,4},{250,5},{249,6},{248,7},{2... | collective-permute-start | bytes 1376264 | tf_op jit(solution)/shard_map/ppermute | solution.py:398
  24.3 12.2 %collective-permute-done.held = f32[9,32,512]{2,1,0:T(8,128)} collective-permute-done((f32[9,32,512]{2,1,0:T(8,128)}, f32[9,32,512]{2,1,0:T(8,128)}, u32[]{:S(2)}, u32[]{:S(2)}) %collective-permute-start) | collective-permute-done | bytes 589856 | tf_op jit(solution)/shard_map/ppermute | solution.py:389
  36.6 1.7 %collective-permute-start.1 = (f32[9,32,512]{2,1,0:T(8,128)}, f32[9,32,512]{2,1,0:T(8,128)}, u32[]{:S(2)}, u32[]{:S(2)}) collective-permute-start(f32[9,32,512]{2,1,0:T(8,128)} %collective-permute-done.held), channel_id=1, source_target_pairs={{224,0},{192,32},{160,64},{128,96},{96,128},{64,160},{32,192},{0,2... | collective-permute-start | bytes 1769480 | tf_op jit(solution)/shard_map/ppermute | solution.py:402
  38.3 0.0 all-to-all-done.received
  38.3 1.2 copy-done.1
  39.5 2.7 %x_forward.1 = f32[32,9,8,128]{3,2,1,0:T(8,128)} custom-call(f32[8,136,128]{2,1,0:T(8,128)S(1)} %all-to-all-done.received, f32[9,32,512]{2,1,0:T(8,128)} %collective-permute-done.held, bf16[1024,512]{1,0:T(8,128)(2,1)S(1)} %copy-done.1), custom_call_target="tpu_custom_call" | custom-call | tf_op jit(solution)/shard_map/x_forward/pallas_call | solution.py:443
  42.2 10.3 %all-to-all-start.1 = ((f32[32,9,8,128]{3,2,1,0:T(8,128)}), f32[32,9,8,128]{3,2,1,0:T(8,128)S(1)}, u32[]{:S(2)}, u32[]{:S(2)}) async-start(f32[32,9,8,128]{3,2,1,0:T(8,128)} %x_forward.1), calls=%async_computation.1 | async-start | bytes 2359296 | tf_op jit(solution)/shard_map/all_to_all | solution.py:451
  52.5 0.0 copy-start.4
  52.5 0.9 copy-done.4
  53.5 0.9 copy-done.7
  54.4 1.6 %copy-done.9 = f32[16,64,512]{2,1,0:T(8,128)S(1)} copy-done((f32[16,64,512]{2,1,0:T(8,128)S(1)}, f32[16,64,512]{2,1,0:T(8,128)}, u32[]{:S(2)}) %copy-start.9) | copy-done | bytes 2097176
  56.0 0.7 own_weights.1
  56.7 0.0 collective-permute-done.2.near
  56.7 1.5 %slice.4 = f32[1,32,512]{2,1,0:T(8,128)} slice(f32[7,32,512]{2,1,0:T(8,128)} %collective-permute-done.2.near), slice={[6:7], [0:32], [0:512]} | slice | bytes 131072 | tf_op jit(solution)/shard_map/slice | solution.py:418
  58.2 2.9 %collective-permute-start.3 = (f32[1,32,512]{2,1,0:T(8,128)}, f32[1,32,512]{2,1,0:T(8,128)}, u32[]{:S(2)}, u32[]{:S(2)}) collective-permute-start(f32[1,32,512]{2,1,0:T(8,128)} %slice.4), channel_id=1, source_target_pairs={{0,1},{1,2},{2,3},{3,4},{4,5},{5,6},{6,7},{7,8},{8,9},{9,10},{10,1... | collective-permute-start | bytes 196616 | tf_op jit(solution)/shard_map/ppermute | solution.py:393
  61.1 10.1 %all-to-all-done.1 = f32[32,9,8,128]{3,2,1,0:T(8,128)S(1)} async-done(((f32[32,9,8,128]{3,2,1,0:T(8,128)}), f32[32,9,8,128]{3,2,1,0:T(8,128)S(1)}, u32[]{:S(2)}, u32[]{:S(2)}) %all-to-all-start.1) | async-done | bytes 1179680 | tf_op jit(solution)/shard_map/all_to_all | solution.py:451
  71.2 1.2 copy-done.2
  72.5 2.3 %y_forward.1.spectrum = f32[512,1152]{1,0:T(8,128)S(1)} custom-call(f32[2304,128]{1,0:T(8,128)S(1)} %bitcast.1, bf16[1024,512]{1,0:T(8,128)(2,1)S(1)} %copy-done.2), custom_call_target="tpu_custom_call" | custom-call | flops 5000000000 | bytes 8388608 | tf_op jit(solution)/shard_map/y_forward/pallas_call | solution.py:452
  74.8 0.0 collective-permute-done.3.rim
  74.8 0.0 collective-permute-done.1.far
  74.8 3.8 %y_inverse.1 = f32[32,8,1152]{2,1,0:T(8,128)S(1)} custom-call(f32[512,1152]{1,0:T(8,128)S(1)} %y_forward.1.spectrum, f32[512,1152]{1,0:T(8,128)S(1)} %get-tuple-element.7.base, f32[9,32,512]{2,1,0:T(8,128)} %collective-permute-done.1.far, f32[7,32,512]{2,1,0:T(8,128)} %collective-permute-done.2.near, f32[1,32,512]{2,1,0:T(8,128)} %collective-permute-done.3.rim, ...), custom_call_target="tpu_custom_call" | custom-call | tf_op jit(solution)/shard_map/y_inverse/pallas_call | solution.py:461
  78.6 0.0 copy-start.3
  78.7 25.0 %all_to_all.20.received = f32[32,8,1152]{2,1,0:T(8,128)S(1)} all-to-all(f32[32,8,1152]{2,1,0:T(8,128)S(1)} %y_inverse.1), channel_id=1, replica_groups=mesh['gx'=8,'gy'=4,'gz'=8] {'gy','gz'}, dimensions={0} | all-to-all | bytes 2359296 | tf_op jit(solution)/shard_map/all_to_all | solution.py:469
  103.7 1.7 %x_inverse.1 = f32[8,136,128]{2,1,0:T(8,128)S(1)} custom-call(f32[32,8,1152]{2,1,0:T(8,128)S(1)} %all_to_all.20.received, bf16[512,1024]{1,0:T(8,128)(2,1)S(1)} %copy-done.3, bf16[512,1024]{1,0:T(8,128)(2,1)S(1)} %copy-done), custom_call_target="tpu_custom_call" | custom-call | tf_op jit(solution)/shard_map/x_inverse/pallas_call | solution.py:470
  105.4 0.0 copy-start.5
  105.4 0.0 copy-start.8
  105.4 26.6 %all_to_all.21.received = f32[8,136,128]{2,1,0:T(8,128)S(1)} all-to-all(f32[8,136,128]{2,1,0:T(8,128)S(1)} %x_inverse.1), channel_id=1, replica_groups=mesh['gx'=8,'gy'=4,'gz'=8] {'gx'}, dimensions={0} | all-to-all | bytes 1114112 | tf_op jit(solution)/shard_map/all_to_all | solution.py:478
  132.1 1.3 %z_inverse.1 = (f32[32,8,256]{2,1,0:T(8,128)}, f32[1]{0:T(128)}) custom-call(f32[8,136,128]{2,1,0:T(8,128)S(1)} %all_to_all.21.received, f32[32,8,256]{2,1,0:T(8,128)S(1)} %copy-done.5, f32[32,8,256]{2,1,0:T(8,128)S(1)} %copy-done.8, bf16[1920,256]{1,0:T(8,128)(2,1)S(1)} %copy-done.6), custom_call_target="tpu_custom_call" | custom-call | tf_op jit(solution)/shard_map/z_inverse/pallas_call | solution.py:479
  (11 shorter events, 0.0 us)
Async XLA Ops:
  3.4 34.9 %all-to-all-start = ((f32[8,136,128]{2,1,0:T(8,128)}), f32[8,136,128]{2,1,0:T(8,128)S(1)}, u32[]{:S(2)}, u32[]{:S(2)}) async-start(f32[8,136,128]{2,1,0:T(8,128)} %z_forward.1), calls=%async_computation | async-start | bytes 1114112 | tf_op jit(solution)/shard_map/all_to_all | solution.py:441
  15.7 20.9 %collective-permute-start = (f32[9,32,512]{2,1,0:T(8,128)}, f32[9,32,512]{2,1,0:T(8,128)}, u32[]{:S(2)}, u32[]{:S(2)}) collective-permute-start(f32[9,32,512]{2,1,0:T(8,128)} %get-tuple-element.6), channel_id=1, source_target_pairs={{31,0},{30,1},{29,2},{28,3},{27,4},{26,5},{25,6},{24,7},{23,8},{22... | collective-permute-start | bytes 1769480 | tf_op jit(solution)/shard_map/ppermute | solution.py:389
  21.6 35.2 %collective-permute-start.2 = (f32[7,32,512]{2,1,0:T(8,128)}, f32[7,32,512]{2,1,0:T(8,128)}, u32[]{:S(2)}, u32[]{:S(2)}) collective-permute-start(f32[7,32,512]{2,1,0:T(8,128)} %get-tuple-element.8), channel_id=1, source_target_pairs={{255,0},{254,1},{253,2},{252,3},{251,4},{250,5},{249,6},{248,7},{2... | collective-permute-start | bytes 1376264 | tf_op jit(solution)/shard_map/ppermute | solution.py:398
  36.6 38.3 %collective-permute-start.1 = (f32[9,32,512]{2,1,0:T(8,128)}, f32[9,32,512]{2,1,0:T(8,128)}, u32[]{:S(2)}, u32[]{:S(2)}) collective-permute-start(f32[9,32,512]{2,1,0:T(8,128)} %collective-permute-done.held), channel_id=1, source_target_pairs={{224,0},{192,32},{160,64},{128,96},{96,128},{64,160},{32,192},{0,2... | collective-permute-start | bytes 1769480 | tf_op jit(solution)/shard_map/ppermute | solution.py:402
  38.3 1.2 copy-start.1
  42.2 29.0 %all-to-all-start.1 = ((f32[32,9,8,128]{3,2,1,0:T(8,128)}), f32[32,9,8,128]{3,2,1,0:T(8,128)S(1)}, u32[]{:S(2)}, u32[]{:S(2)}) async-start(f32[32,9,8,128]{3,2,1,0:T(8,128)} %x_forward.1), calls=%async_computation.1 | async-start | bytes 2359296 | tf_op jit(solution)/shard_map/all_to_all | solution.py:451
  52.5 1.0 copy-start.4
  53.5 0.9 copy-start.7
  54.4 1.6 %copy-start.9 = (f32[16,64,512]{2,1,0:T(8,128)S(1)}, f32[16,64,512]{2,1,0:T(8,128)}, u32[]{:S(2)}) copy-start(f32[16,64,512]{2,1,0:T(8,128)} %own.3) | copy-start | bytes 6291460
  58.2 16.6 %collective-permute-start.3 = (f32[1,32,512]{2,1,0:T(8,128)}, f32[1,32,512]{2,1,0:T(8,128)}, u32[]{:S(2)}, u32[]{:S(2)}) collective-permute-start(f32[1,32,512]{2,1,0:T(8,128)} %slice.4), channel_id=1, source_target_pairs={{0,1},{1,2},{2,3},{3,4},{4,5},{5,6},{6,7},{7,8},{8,9},{9,10},{10,1... | collective-permute-start | bytes 196616 | tf_op jit(solution)/shard_map/ppermute | solution.py:393
  71.2 1.2 copy-start.2
  72.5 2.4 %copy-start = (bf16[512,1024]{1,0:T(8,128)(2,1)S(1)}, bf16[512,1024]{1,0:T(8,128)(2,1)}, u32[]{:S(2)}) copy-start(bf16[512,1024]{1,0:T(8,128)(2,1)} %constant.12.clone.table.plain) | copy-start | bytes 3145732
  78.6 25.0 %copy-start.3 = (bf16[512,1024]{1,0:T(8,128)(2,1)S(1)}, bf16[512,1024]{1,0:T(8,128)(2,1)}, u32[]{:S(2)}) copy-start(bf16[512,1024]{1,0:T(8,128)(2,1)} %constant.13.clone.table) | copy-start | bytes 3145732
  103.7 28.4 %copy-start.6 = (bf16[1920,256]{1,0:T(8,128)(2,1)S(1)}, bf16[1920,256]{1,0:T(8,128)(2,1)}, u32[]{:S(2)}) copy-start(bf16[1920,256]{1,0:T(8,128)(2,1)} %constant.14.clone.table) | copy-start | bytes 2949124
  105.4 26.6 %copy-start.5 = (f32[32,8,256]{2,1,0:T(8,128)S(1)}, f32[32,8,256]{2,1,0:T(8,128)}, u32[]{:S(2)}) copy-start(f32[32,8,256]{2,1,0:T(8,128)} %volume.5) | copy-start | bytes 786436
  105.4 26.6 %copy-start.8 = (f32[32,8,256]{2,1,0:T(8,128)S(1)}, f32[32,8,256]{2,1,0:T(8,128)}, u32[]{:S(2)}) copy-start(f32[32,8,256]{2,1,0:T(8,128)} %prior.3) | copy-start | bytes 786436

commit v4 on v3

--- a/solution.py
+++ b/solution.py
@@ -50,7 +50,7 @@
     stacked = np.stack([cosine, -sine], axis=0).reshape(2, GX // 2, 2, 64, M)
     main = stacked[:, :, :, :HALF].transpose(1, 0, 2, 3, 4).reshape(GX * 64, M)
     edge = stacked[:, :, :, HALF].transpose(1, 2, 0, 3).reshape(GX * 2, M)
-    return stack_right(np.concatenate([main, np.repeat(edge, 8, axis=0)], axis=0) / float(N) ** 3)
+    return stack_left(np.concatenate([main, np.repeat(edge, 8, axis=0)], axis=0) / float(N) ** 3)
 
 
 def forward_table():
@@ -81,11 +81,6 @@
 
 def stack_left(table):
     return np.concatenate(halves(table), axis=0)
-
-
-def stack_right(table):
-    high, low = halves(table)
-    return np.concatenate([high, low, high], axis=0)
 
 
 def table_dot(table, data):
@@ -97,7 +92,9 @@
 
 def data_dot(data, table):
     high, low = split(data)
-    return dot(jnp.concatenate([high, high, low], axis=1), table[...])
+    count, depth = data.shape
+    wide = dot(jnp.concatenate([high, low], axis=0), table[:depth])
+    return wide[:count] + (wide[count:] + dot(high, table[depth:]))
 
 
 def rotated(value, sign):

time: 134 us -> 134 us (level)
  no operation moved by 1% of the time
where the time goes in v4:
time: 134 us
  blocking collectives  51.6 us (39%)
  starting transfers between devices  32.5 us (24%)
  waiting for transfers between devices  22.4 us (17%)
  Pallas kernels  18.7 us (14%)
  local copies, waits for them, and re-layouts  7.44 us (6%)
    all_to_all x1, blocking collectives, local(): got = lax.all_to_all(sent, 'gx', split_axis=0, concat_axis=0, tiled=True)  26.6 us
    all_to_all x1, blocking collectives, local(): lax.all_to_all(sent, ('gy', 'gz'), split_axis=0, concat_axis=0, tiled=True)  25 us
    ppermute x1, waiting for transfers between devices, mirror(): return lax.ppermute(value, ('gy', 'gz'), pairs)  12.2 us
    all_to_all x1, starting transfers between devices, local(): lax.all_to_all(sent, ('gy', 'gz'), split_axis=0, concat_axis=0, tiled=True)  10.3 us
    all_to_all x1, waiting for transfers between devices, local(): lax.all_to_all(sent, ('gy', 'gz'), split_axis=0, concat_axis=0, tiled=True)  10.1 us
    all_to_all x1, starting transfers between devices, local(): got = lax.all_to_all(sent, 'gx', split_axis=0, concat_axis=0, tiled=True)  9.03 us
    unnamed x20, local copies, waits for them, and re-layouts  5.96 us
    ppermute x1, starting transfers between devices, mirror(): return lax.ppermute(value, ('gy', 'gz'), pairs)  5.86 us
  transfers between devices with their start and end apart: 6, of which 2 were waited for; matrix products, arithmetic and copies ran while one was open for 1% of the time, Pallas kernels for 7%

profile of v4, /device:TPU:1, one launch (start us, length us, event | category | flops | bytes accessed | tf_op | source)
XLA Modules:
  0.0 133.6 jit_solution(662026005307666708)
XLA Ops:
  0.6 2.7 %z_forward.1 = f32[8,136,128]{2,1,0:T(8,128)} custom-call(f32[32,8,256]{2,1,0:T(8,128)} %volume.5, bf16[512,640]{1,0:T(8,128)(2,1)} %constant.10.clone.table), custom_call_target="tpu_custom_call" | custom-call | tf_op jit(solution)/shard_map/z_forward/pallas_call | solution.py:425
  3.4 9.0 %all-to-all-start = ((f32[8,136,128]{2,1,0:T(8,128)}), f32[8,136,128]{2,1,0:T(8,128)S(1)}, u32[]{:S(2)}, u32[]{:S(2)}) async-start(f32[8,136,128]{2,1,0:T(8,128)} %z_forward.1), calls=%async_computation | async-start | bytes 1114112 | tf_op jit(solution)/shard_map/all_to_all | solution.py:438
  12.4 3.3 %turn.1 = (f32[9,32,512]{2,1,0:T(8,128)}, f32[7,32,512]{2,1,0:T(8,128)}) custom-call(f32[16,64,512]{2,1,0:T(8,128)} %own.3), custom_call_target="tpu_custom_call" | custom-call | flops 8000000000 | bytes 8388608 | tf_op jit(solution)/shard_map/turn/pallas_call | solution.py:403
  15.7 5.9 %collective-permute-start = (f32[9,32,512]{2,1,0:T(8,128)}, f32[9,32,512]{2,1,0:T(8,128)}, u32[]{:S(2)}, u32[]{:S(2)}) collective-permute-start(f32[9,32,512]{2,1,0:T(8,128)} %get-tuple-element.6), channel_id=1, source_target_pairs={{31,0},{30,1},{29,2},{28,3},{27,4},{26,5},{25,6},{24,7},{23,8},{22... | collective-permute-start | bytes 1769480 | tf_op jit(solution)/shard_map/ppermute | solution.py:386
  21.6 2.8 %collective-permute-start.2 = (f32[7,32,512]{2,1,0:T(8,128)}, f32[7,32,512]{2,1,0:T(8,128)}, u32[]{:S(2)}, u32[]{:S(2)}) collective-permute-start(f32[7,32,512]{2,1,0:T(8,128)} %get-tuple-element.8), channel_id=1, source_target_pairs={{255,0},{254,1},{253,2},{252,3},{251,4},{250,5},{249,6},{248,7},{2... | collective-permute-start | bytes 1376264 | tf_op jit(solution)/shard_map/ppermute | solution.py:395
  24.3 12.2 %collective-permute-done.held = f32[9,32,512]{2,1,0:T(8,128)} collective-permute-done((f32[9,32,512]{2,1,0:T(8,128)}, f32[9,32,512]{2,1,0:T(8,128)}, u32[]{:S(2)}, u32[]{:S(2)}) %collective-permute-start) | collective-permute-done | bytes 589856 | tf_op jit(solution)/shard_map/ppermute | solution.py:386
  36.6 1.7 %collective-permute-start.1 = (f32[9,32,512]{2,1,0:T(8,128)}, f32[9,32,512]{2,1,0:T(8,128)}, u32[]{:S(2)}, u32[]{:S(2)}) collective-permute-start(f32[9,32,512]{2,1,0:T(8,128)} %collective-permute-done.held), channel_id=1, source_target_pairs={{224,0},{192,32},{160,64},{128,96},{96,128},{64,160},{32,192},{0,2... | collective-permute-start | bytes 1769480 | tf_op jit(solution)/shard_map/ppermute | solution.py:399
  38.3 0.0 all-to-all-done.received
  38.3 1.2 copy-done.1
  39.5 2.7 %x_forward.1 = f32[32,9,8,128]{3,2,1,0:T(8,128)} custom-call(f32[8,136,128]{2,1,0:T(8,128)S(1)} %all-to-all-done.received, f32[9,32,512]{2,1,0:T(8,128)} %collective-permute-done.held, bf16[1024,512]{1,0:T(8,128)(2,1)S(1)} %copy-done.1), custom_call_target="tpu_custom_call" | custom-call | tf_op jit(solution)/shard_map/x_forward/pallas_call | solution.py:440
  42.2 10.3 %all-to-all-start.1 = ((f32[32,9,8,128]{3,2,1,0:T(8,128)}), f32[32,9,8,128]{3,2,1,0:T(8,128)S(1)}, u32[]{:S(2)}, u32[]{:S(2)}) async-start(f32[32,9,8,128]{3,2,1,0:T(8,128)} %x_forward.1), calls=%async_computation.1 | async-start | bytes 2359296 | tf_op jit(solution)/shard_map/all_to_all | solution.py:448
  52.5 0.0 copy-start.4
  52.5 0.9 copy-done.4
  53.5 0.9 copy-done.7
  54.4 1.6 %copy-done.9 = f32[16,64,512]{2,1,0:T(8,128)S(1)} copy-done((f32[16,64,512]{2,1,0:T(8,128)S(1)}, f32[16,64,512]{2,1,0:T(8,128)}, u32[]{:S(2)}) %copy-start.9) | copy-done | bytes 2097176
  56.0 0.7 own_weights.1
  56.7 0.0 collective-permute-done.2.near
  56.7 1.5 %slice.4 = f32[1,32,512]{2,1,0:T(8,128)} slice(f32[7,32,512]{2,1,0:T(8,128)} %collective-permute-done.2.near), slice={[6:7], [0:32], [0:512]} | slice | bytes 131072 | tf_op jit(solution)/shard_map/slice | solution.py:415
  58.2 2.9 %collective-permute-start.3 = (f32[1,32,512]{2,1,0:T(8,128)}, f32[1,32,512]{2,1,0:T(8,128)}, u32[]{:S(2)}, u32[]{:S(2)}) collective-permute-start(f32[1,32,512]{2,1,0:T(8,128)} %slice.4), channel_id=1, source_target_pairs={{0,1},{1,2},{2,3},{3,4},{4,5},{5,6},{6,7},{7,8},{8,9},{9,10},{10,1... | collective-permute-start | bytes 196616 | tf_op jit(solution)/shard_map/ppermute | solution.py:390
  61.1 10.1 %all-to-all-done.1 = f32[32,9,8,128]{3,2,1,0:T(8,128)S(1)} async-done(((f32[32,9,8,128]{3,2,1,0:T(8,128)}), f32[32,9,8,128]{3,2,1,0:T(8,128)S(1)}, u32[]{:S(2)}, u32[]{:S(2)}) %all-to-all-start.1) | async-done | bytes 1179680 | tf_op jit(solution)/shard_map/all_to_all | solution.py:448
  71.2 1.2 copy-done.2
  72.5 2.3 %y_forward.1.spectrum = f32[512,1152]{1,0:T(8,128)S(1)} custom-call(f32[2304,128]{1,0:T(8,128)S(1)} %bitcast.1, bf16[1024,512]{1,0:T(8,128)(2,1)S(1)} %copy-done.2), custom_call_target="tpu_custom_call" | custom-call | flops 5000000000 | bytes 8388608 | tf_op jit(solution)/shard_map/y_forward/pallas_call | solution.py:449
  74.8 0.0 collective-permute-done.3.rim
  74.8 0.0 collective-permute-done.1.far
  74.8 3.8 %y_inverse.1 = f32[32,8,1152]{2,1,0:T(8,128)S(1)} custom-call(f32[512,1152]{1,0:T(8,128)S(1)} %y_forward.1.spectrum, f32[512,1152]{1,0:T(8,128)S(1)} %get-tuple-element.7.base, f32[9,32,512]{2,1,0:T(8,128)} %collective-permute-done.1.far, f32[7,32,512]{2,1,0:T(8,128)} %collective-permute-done.2.near, f32[1,32,512]{2,1,0:T(8,128)} %collective-permute-done.3.rim, ...), custom_call_target="tpu_custom_call" | custom-call | tf_op jit(solution)/shard_map/y_inverse/pallas_call | solution.py:458
  78.6 0.0 copy-start.3
  78.7 25.0 %all_to_all.20.received = f32[32,8,1152]{2,1,0:T(8,128)S(1)} all-to-all(f32[32,8,1152]{2,1,0:T(8,128)S(1)} %y_inverse.1), channel_id=1, replica_groups=mesh['gx'=8,'gy'=4,'gz'=8] {'gy','gz'}, dimensions={0} | all-to-all | bytes 2359296 | tf_op jit(solution)/shard_map/all_to_all | solution.py:466
  103.7 1.7 %x_inverse.1 = f32[8,136,128]{2,1,0:T(8,128)S(1)} custom-call(f32[32,8,1152]{2,1,0:T(8,128)S(1)} %all_to_all.20.received, bf16[512,1024]{1,0:T(8,128)(2,1)S(1)} %copy-done.3, bf16[512,1024]{1,0:T(8,128)(2,1)S(1)} %copy-done), custom_call_target="tpu_custom_call" | custom-call | tf_op jit(solution)/shard_map/x_inverse/pallas_call | solution.py:467
  105.4 0.0 copy-start.5
  105.4 0.0 copy-start.6
  105.4 26.6 %all_to_all.21.received = f32[8,136,128]{2,1,0:T(8,128)S(1)} all-to-all(f32[8,136,128]{2,1,0:T(8,128)S(1)} %x_inverse.1), channel_id=1, replica_groups=mesh['gx'=8,'gy'=4,'gz'=8] {'gx'}, dimensions={0} | all-to-all | bytes 1114112 | tf_op jit(solution)/shard_map/all_to_all | solution.py:475
  132.1 1.4 %z_inverse.1 = (f32[32,8,256]{2,1,0:T(8,128)}, f32[1]{0:T(128)}) custom-call(f32[8,136,128]{2,1,0:T(8,128)S(1)} %all_to_all.21.received, f32[32,8,256]{2,1,0:T(8,128)S(1)} %copy-done.5, f32[32,8,256]{2,1,0:T(8,128)S(1)} %copy-done.8, bf16[1280,256]{1,0:T(8,128)(2,1)S(1)} %copy-done.6), custom_call_target="tpu_custom_call" | custom-call | tf_op jit(solution)/shard_map/z_inverse/pallas_call | solution.py:476
  (11 shorter events, 0.0 us)
Async XLA Ops:
  3.4 34.9 %all-to-all-start = ((f32[8,136,128]{2,1,0:T(8,128)}), f32[8,136,128]{2,1,0:T(8,128)S(1)}, u32[]{:S(2)}, u32[]{:S(2)}) async-start(f32[8,136,128]{2,1,0:T(8,128)} %z_forward.1), calls=%async_computation | async-start | bytes 1114112 | tf_op jit(solution)/shard_map/all_to_all | solution.py:438
  15.7 20.9 %collective-permute-start = (f32[9,32,512]{2,1,0:T(8,128)}, f32[9,32,512]{2,1,0:T(8,128)}, u32[]{:S(2)}, u32[]{:S(2)}) collective-permute-start(f32[9,32,512]{2,1,0:T(8,128)} %get-tuple-element.6), channel_id=1, source_target_pairs={{31,0},{30,1},{29,2},{28,3},{27,4},{26,5},{25,6},{24,7},{23,8},{22... | collective-permute-start | bytes 1769480 | tf_op jit(solution)/shard_map/ppermute | solution.py:386
  21.6 35.2 %collective-permute-start.2 = (f32[7,32,512]{2,1,0:T(8,128)}, f32[7,32,512]{2,1,0:T(8,128)}, u32[]{:S(2)}, u32[]{:S(2)}) collective-permute-start(f32[7,32,512]{2,1,0:T(8,128)} %get-tuple-element.8), channel_id=1, source_target_pairs={{255,0},{254,1},{253,2},{252,3},{251,4},{250,5},{249,6},{248,7},{2... | collective-permute-start | bytes 1376264 | tf_op jit(solution)/shard_map/ppermute | solution.py:395
  36.6 38.3 %collective-permute-start.1 = (f32[9,32,512]{2,1,0:T(8,128)}, f32[9,32,512]{2,1,0:T(8,128)}, u32[]{:S(2)}, u32[]{:S(2)}) collective-permute-start(f32[9,32,512]{2,1,0:T(8,128)} %collective-permute-done.held), channel_id=1, source_target_pairs={{224,0},{192,32},{160,64},{128,96},{96,128},{64,160},{32,192},{0,2... | collective-permute-start | bytes 1769480 | tf_op jit(solution)/shard_map/ppermute | solution.py:399
  38.3 1.2 copy-start.1
  42.2 29.0 %all-to-all-start.1 = ((f32[32,9,8,128]{3,2,1,0:T(8,128)}), f32[32,9,8,128]{3,2,1,0:T(8,128)S(1)}, u32[]{:S(2)}, u32[]{:S(2)}) async-start(f32[32,9,8,128]{3,2,1,0:T(8,128)} %x_forward.1), calls=%async_computation.1 | async-start | bytes 2359296 | tf_op jit(solution)/shard_map/all_to_all | solution.py:448
  52.5 1.0 copy-start.4
  53.5 0.9 copy-start.7
  54.4 1.6 %copy-start.9 = (f32[16,64,512]{2,1,0:T(8,128)S(1)}, f32[16,64,512]{2,1,0:T(8,128)}, u32[]{:S(2)}) copy-start(f32[16,64,512]{2,1,0:T(8,128)} %own.3) | copy-start | bytes 6291460
  58.2 16.6 %collective-permute-start.3 = (f32[1,32,512]{2,1,0:T(8,128)}, f32[1,32,512]{2,1,0:T(8,128)}, u32[]{:S(2)}, u32[]{:S(2)}) collective-permute-start(f32[1,32,512]{2,1,0:T(8,128)} %slice.4), channel_id=1, source_target_pairs={{0,1},{1,2},{2,3},{3,4},{4,5},{5,6},{6,7},{7,8},{8,9},{9,10},{10,1... | collective-permute-start | bytes 196616 | tf_op jit(solution)/shard_map/ppermute | solution.py:390
  71.2 1.2 copy-start.2
  72.5 2.4 %copy-start = (bf16[512,1024]{1,0:T(8,128)(2,1)S(1)}, bf16[512,1024]{1,0:T(8,128)(2,1)}, u32[]{:S(2)}) copy-start(bf16[512,1024]{1,0:T(8,128)(2,1)} %constant.12.clone.table.plain) | copy-start | bytes 3145732
  78.6 25.0 %copy-start.3 = (bf16[512,1024]{1,0:T(8,128)(2,1)S(1)}, bf16[512,1024]{1,0:T(8,128)(2,1)}, u32[]{:S(2)}) copy-start(bf16[512,1024]{1,0:T(8,128)(2,1)} %constant.13.clone.table) | copy-start | bytes 3145732
  103.7 28.4 %copy-start.8 = (f32[32,8,256]{2,1,0:T(8,128)S(1)}, f32[32,8,256]{2,1,0:T(8,128)}, u32[]{:S(2)}) copy-start(f32[32,8,256]{2,1,0:T(8,128)} %prior.3) | copy-start | bytes 786436
  105.4 26.6 %copy-start.5 = (f32[32,8,256]{2,1,0:T(8,128)S(1)}, f32[32,8,256]{2,1,0:T(8,128)}, u32[]{:S(2)}) copy-start(f32[32,8,256]{2,1,0:T(8,128)} %volume.5) | copy-start | bytes 786436
  105.4 26.6 %copy-start.6 = (bf16[1280,256]{1,0:T(8,128)(2,1)S(1)}, bf16[1280,256]{1,0:T(8,128)(2,1)}, u32[]{:S(2)}) copy-start(bf16[1280,256]{1,0:T(8,128)(2,1)} %constant.14.clone.table) | copy-start | bytes 1966084

commit v5 on v3

--- a/solution.py
+++ b/solution.py
@@ -14,7 +14,7 @@
 GX = 8
 GA = 32
 HALF = 32
-EARLY = 6
+EARLY = 7
 LATE = 15 - EARLY
 OWN_COST = 20
 TURN_COST = 8

time: 134 us -> 134 us (level)
  blocking collectives: 51.6 us -> 48.8 us
  waiting for transfers between devices: 22.4 us -> 25.2 us
    ppermute x1, waiting for transfers between devices: 0.01 us -> 10.4 us  [reflect(): lax.ppermute(value, AXES, [(count - 1 - at, at) for at in range(count)])]
    all_to_all x1, waiting for transfers between devices: 10.1 us -> 2.42 us  [local(): lax.all_to_all(sent, ('gy', 'gz'), split_axis=0, concat_axis=0, tiled=True)]
    all_to_all x1, starting transfers between devices: 10.3 us -> 13.1 us  [local(): lax.all_to_all(sent, ('gy', 'gz'), split_axis=0, concat_axis=0, tiled=True)]
    ppermute x1, starting transfers between devices: 2.89 us -> 0.16 us  [onward(): lax.ppermute(value, ('gy', 'gz'), [(group, (group + 1) % GA) for group in...]
    ppermute x1, waiting for transfers between devices: 0.01 us -> 1.47 us  [onward(): lax.ppermute(value, ('gy', 'gz'), [(group, (group + 1) % GA) for group in...]
    all_to_all x1, blocking collectives: 26.6 us -> 25.2 us  [local(): got = lax.all_to_all(sent, 'gx', split_axis=0, concat_axis=0, tiled=True)]
    ppermute x1, waiting for transfers between devices: 12.2 us -> 10.8 us  [mirror(): return lax.ppermute(value, ('gy', 'gz'), pairs)]
    all_to_all x1, blocking collectives: 25 us -> 23.6 us  [local(): lax.all_to_all(sent, ('gy', 'gz'), split_axis=0, concat_axis=0, tiled=True)]
  transfers between devices with their start and end apart: 6 -> 6, of which waited for: 2 -> 4; matrix products, arithmetic and copies ran while one was open for 1% -> 1% of each run, Pallas kernels for 7% -> 7%
where the time goes in v5:
time: 134 us
  blocking collectives  48.8 us (36%)
  starting transfers between devices  32.6 us (24%)
  waiting for transfers between devices  25.2 us (19%)
  Pallas kernels  18.7 us (14%)
  local copies, waits for them, and re-layouts  7.44 us (6%)
    all_to_all x1, blocking collectives, local(): got = lax.all_to_all(sent, 'gx', split_axis=0, concat_axis=0, tiled=True)  25.2 us
    all_to_all x1, blocking collectives, local(): lax.all_to_all(sent, ('gy', 'gz'), split_axis=0, concat_axis=0, tiled=True)  23.6 us
    all_to_all x1, starting transfers between devices, local(): lax.all_to_all(sent, ('gy', 'gz'), split_axis=0, concat_axis=0, tiled=True)  13.1 us
    ppermute x1, waiting for transfers between devices, mirror(): return lax.ppermute(value, ('gy', 'gz'), pairs)  10.8 us
    ppermute x1, waiting for transfers between devices, reflect(): lax.ppermute(value, AXES, [(count - 1 - at, at) for at in range(count)])  10.4 us
    all_to_all x1, starting transfers between devices, local(): got = lax.all_to_all(sent, 'gx', split_axis=0, concat_axis=0, tiled=True)  9.03 us
    unnamed x20, local copies, waits for them, and re-layouts  5.96 us
    ppermute x1, starting transfers between devices, mirror(): return lax.ppermute(value, ('gy', 'gz'), pairs)  5.85 us
  transfers between devices with their start and end apart: 6, of which 4 were waited for; matrix products, arithmetic and copies ran while one was open for 1% of the time, Pallas kernels for 7%

profile of v5, /device:TPU:1, one launch (start us, length us, event | category | flops | bytes accessed | tf_op | source)
XLA Modules:
  0.0 133.6 jit_solution(7828295041858653400)
XLA Ops:
  0.6 2.7 %z_forward.1 = f32[8,136,128]{2,1,0:T(8,128)} custom-call(f32[32,8,256]{2,1,0:T(8,128)} %volume.5, bf16[512,640]{1,0:T(8,128)(2,1)} %constant.10.clone.table), custom_call_target="tpu_custom_call" | custom-call | tf_op jit(solution)/shard_map/z_forward/pallas_call | solution.py:428
  3.4 9.0 %all-to-all-start = ((f32[8,136,128]{2,1,0:T(8,128)}), f32[8,136,128]{2,1,0:T(8,128)S(1)}, u32[]{:S(2)}, u32[]{:S(2)}) async-start(f32[8,136,128]{2,1,0:T(8,128)} %z_forward.1), calls=%async_computation | async-start | bytes 1114112 | tf_op jit(solution)/shard_map/all_to_all | solution.py:441
  12.4 3.3 %turn.1 = (f32[8,32,512]{2,1,0:T(8,128)}, f32[8,32,512]{2,1,0:T(8,128)}) custom-call(f32[16,64,512]{2,1,0:T(8,128)} %own.3), custom_call_target="tpu_custom_call" | custom-call | flops 8000000000 | bytes 8388608 | tf_op jit(solution)/shard_map/turn/pallas_call | solution.py:406
  15.7 5.8 %collective-permute-start = (f32[8,32,512]{2,1,0:T(8,128)}, f32[8,32,512]{2,1,0:T(8,128)}, u32[]{:S(2)}, u32[]{:S(2)}) collective-permute-start(f32[8,32,512]{2,1,0:T(8,128)} %get-tuple-element.6), channel_id=1, source_target_pairs={{31,0},{30,1},{29,2},{28,3},{27,4},{26,5},{25,6},{24,7},{23,8},{22... | collective-permute-start | bytes 1572872 | tf_op jit(solution)/shard_map/ppermute | solution.py:389
  21.6 2.8 %collective-permute-start.2 = (f32[8,32,512]{2,1,0:T(8,128)}, f32[8,32,512]{2,1,0:T(8,128)}, u32[]{:S(2)}, u32[]{:S(2)}) collective-permute-start(f32[8,32,512]{2,1,0:T(8,128)} %get-tuple-element.8), channel_id=1, source_target_pairs={{255,0},{254,1},{253,2},{252,3},{251,4},{250,5},{249,6},{248,7},{2... | collective-permute-start | bytes 1572872 | tf_op jit(solution)/shard_map/ppermute | solution.py:398
  24.4 10.8 %collective-permute-done.held = f32[8,32,512]{2,1,0:T(8,128)} collective-permute-done((f32[8,32,512]{2,1,0:T(8,128)}, f32[8,32,512]{2,1,0:T(8,128)}, u32[]{:S(2)}, u32[]{:S(2)}) %collective-permute-start) | collective-permute-done | bytes 524320 | tf_op jit(solution)/shard_map/ppermute | solution.py:389
  35.2 1.7 %collective-permute-start.1 = (f32[8,32,512]{2,1,0:T(8,128)}, f32[8,32,512]{2,1,0:T(8,128)}, u32[]{:S(2)}, u32[]{:S(2)}) collective-permute-start(f32[8,32,512]{2,1,0:T(8,128)} %collective-permute-done.held), channel_id=1, source_target_pairs={{224,0},{192,32},{160,64},{128,96},{96,128},{64,160},{32,192},{0,2... | collective-permute-start | bytes 1572872 | tf_op jit(solution)/shard_map/ppermute | solution.py:402
  36.9 0.0 all-to-all-done.received
  36.9 1.2 copy-done.1
  38.1 2.7 %x_forward.1 = f32[32,9,8,128]{3,2,1,0:T(8,128)} custom-call(f32[8,136,128]{2,1,0:T(8,128)S(1)} %all-to-all-done.received, f32[8,32,512]{2,1,0:T(8,128)} %collective-permute-done.held, bf16[1024,512]{1,0:T(8,128)(2,1)S(1)} %copy-done.1), custom_call_target="tpu_custom_call" | custom-call | tf_op jit(solution)/shard_map/x_forward/pallas_call | solution.py:443
  40.9 13.1 %all-to-all-start.1 = ((f32[32,9,8,128]{3,2,1,0:T(8,128)}), f32[32,9,8,128]{3,2,1,0:T(8,128)S(1)}, u32[]{:S(2)}, u32[]{:S(2)}) async-start(f32[32,9,8,128]{3,2,1,0:T(8,128)} %x_forward.1), calls=%async_computation.1 | async-start | bytes 2359296 | tf_op jit(solution)/shard_map/all_to_all | solution.py:451
  53.9 0.0 copy-start.4
  53.9 0.9 copy-done.4
  54.9 0.9 copy-done.7
  55.8 1.6 %copy-done.9 = f32[16,64,512]{2,1,0:T(8,128)S(1)} copy-done((f32[16,64,512]{2,1,0:T(8,128)S(1)}, f32[16,64,512]{2,1,0:T(8,128)}, u32[]{:S(2)}) %copy-start.9) | copy-done | bytes 2097176
  57.4 0.7 own_weights.1
  58.1 10.4 %collective-permute-done.2.near = f32[8,32,512]{2,1,0:T(8,128)} collective-permute-done((f32[8,32,512]{2,1,0:T(8,128)}, f32[8,32,512]{2,1,0:T(8,128)}, u32[]{:S(2)}, u32[]{:S(2)}) %collective-permute-start.2) | collective-permute-done | bytes 524320 | tf_op jit(solution)/shard_map/ppermute | solution.py:398
  68.6 1.5 %slice.4 = f32[1,32,512]{2,1,0:T(8,128)} slice(f32[8,32,512]{2,1,0:T(8,128)} %collective-permute-done.2.near), slice={[7:8], [0:32], [0:512]} | slice | bytes 131072 | tf_op jit(solution)/shard_map/slice | solution.py:418
  70.1 0.2 collective-permute-start.3
  70.2 2.4 %all-to-all-done.1 = f32[32,9,8,128]{3,2,1,0:T(8,128)S(1)} async-done(((f32[32,9,8,128]{3,2,1,0:T(8,128)}), f32[32,9,8,128]{3,2,1,0:T(8,128)S(1)}, u32[]{:S(2)}, u32[]{:S(2)}) %all-to-all-start.1) | async-done | bytes 1179680 | tf_op jit(solution)/shard_map/all_to_all | solution.py:451
  72.6 1.2 copy-done.2
  73.9 2.3 %y_forward.1.spectrum = f32[512,1152]{1,0:T(8,128)S(1)} custom-call(f32[2304,128]{1,0:T(8,128)S(1)} %bitcast.1, bf16[1024,512]{1,0:T(8,128)(2,1)S(1)} %copy-done.2), custom_call_target="tpu_custom_call" | custom-call | flops 5000000000 | bytes 8388608 | tf_op jit(solution)/shard_map/y_forward/pallas_call | solution.py:452
  76.2 1.5 %collective-permute-done.3.rim = f32[1,32,512]{2,1,0:T(8,128)} collective-permute-done((f32[1,32,512]{2,1,0:T(8,128)}, f32[1,32,512]{2,1,0:T(8,128)}, u32[]{:S(2)}, u32[]{:S(2)}) %collective-permute-start.3) | collective-permute-done | bytes 65568 | tf_op jit(solution)/shard_map/ppermute | solution.py:393
  77.7 0.0 collective-permute-done.1.far
  77.7 3.8 %y_inverse.1 = f32[32,8,1152]{2,1,0:T(8,128)S(1)} custom-call(f32[512,1152]{1,0:T(8,128)S(1)} %y_forward.1.spectrum, f32[512,1152]{1,0:T(8,128)S(1)} %get-tuple-element.7.base, f32[8,32,512]{2,1,0:T(8,128)} %collective-permute-done.1.far, f32[8,32,512]{2,1,0:T(8,128)} %collective-permute-done.2.near, f32[1,32,512]{2,1,0:T(8,128)} %collective-permute-done.3.rim, ...), custom_call_target="tpu_custom_call" | custom-call | tf_op jit(solution)/shard_map/y_inverse/pallas_call | solution.py:461
  81.5 0.0 copy-start.3
  81.5 23.6 %all_to_all.20.received = f32[32,8,1152]{2,1,0:T(8,128)S(1)} all-to-all(f32[32,8,1152]{2,1,0:T(8,128)S(1)} %y_inverse.1), channel_id=1, replica_groups=mesh['gx'=8,'gy'=4,'gz'=8] {'gy','gz'}, dimensions={0} | all-to-all | bytes 2359296 | tf_op jit(solution)/shard_map/all_to_all | solution.py:469
  105.1 1.7 %x_inverse.1 = f32[8,136,128]{2,1,0:T(8,128)S(1)} custom-call(f32[32,8,1152]{2,1,0:T(8,128)S(1)} %all_to_all.20.received, bf16[512,1024]{1,0:T(8,128)(2,1)S(1)} %copy-done.3, bf16[512,1024]{1,0:T(8,128)(2,1)S(1)} %copy-done), custom_call_target="tpu_custom_call" | custom-call | tf_op jit(solution)/shard_map/x_inverse/pallas_call | solution.py:470
  106.9 0.0 copy-start.5
  106.9 0.0 copy-start.8
  106.9 25.2 %all_to_all.21.received = f32[8,136,128]{2,1,0:T(8,128)S(1)} all-to-all(f32[8,136,128]{2,1,0:T(8,128)S(1)} %x_inverse.1), channel_id=1, replica_groups=mesh['gx'=8,'gy'=4,'gz'=8] {'gx'}, dimensions={0} | all-to-all | bytes 1114112 | tf_op jit(solution)/shard_map/all_to_all | solution.py:478
  132.1 1.3 %z_inverse.1 = (f32[32,8,256]{2,1,0:T(8,128)}, f32[1]{0:T(128)}) custom-call(f32[8,136,128]{2,1,0:T(8,128)S(1)} %all_to_all.21.received, f32[32,8,256]{2,1,0:T(8,128)S(1)} %copy-done.5, f32[32,8,256]{2,1,0:T(8,128)S(1)} %copy-done.8, bf16[1920,256]{1,0:T(8,128)(2,1)S(1)} %copy-done.6), custom_call_target="tpu_custom_call" | custom-call | tf_op jit(solution)/shard_map/z_inverse/pallas_call | solution.py:479
  (11 shorter events, 0.0 us)
Async XLA Ops:
  3.4 33.5 %all-to-all-start = ((f32[8,136,128]{2,1,0:T(8,128)}), f32[8,136,128]{2,1,0:T(8,128)S(1)}, u32[]{:S(2)}, u32[]{:S(2)}) async-start(f32[8,136,128]{2,1,0:T(8,128)} %z_forward.1), calls=%async_computation | async-start | bytes 1114112 | tf_op jit(solution)/shard_map/all_to_all | solution.py:441
  15.7 19.4 %collective-permute-start = (f32[8,32,512]{2,1,0:T(8,128)}, f32[8,32,512]{2,1,0:T(8,128)}, u32[]{:S(2)}, u32[]{:S(2)}) collective-permute-start(f32[8,32,512]{2,1,0:T(8,128)} %get-tuple-element.6), channel_id=1, source_target_pairs={{31,0},{30,1},{29,2},{28,3},{27,4},{26,5},{25,6},{24,7},{23,8},{22... | collective-permute-start | bytes 1572872 | tf_op jit(solution)/shard_map/ppermute | solution.py:389
  21.6 47.0 %collective-permute-start.2 = (f32[8,32,512]{2,1,0:T(8,128)}, f32[8,32,512]{2,1,0:T(8,128)}, u32[]{:S(2)}, u32[]{:S(2)}) collective-permute-start(f32[8,32,512]{2,1,0:T(8,128)} %get-tuple-element.8), channel_id=1, source_target_pairs={{255,0},{254,1},{253,2},{252,3},{251,4},{250,5},{249,6},{248,7},{2... | collective-permute-start | bytes 1572872 | tf_op jit(solution)/shard_map/ppermute | solution.py:398
  35.2 42.5 %collective-permute-start.1 = (f32[8,32,512]{2,1,0:T(8,128)}, f32[8,32,512]{2,1,0:T(8,128)}, u32[]{:S(2)}, u32[]{:S(2)}) collective-permute-start(f32[8,32,512]{2,1,0:T(8,128)} %collective-permute-done.held), channel_id=1, source_target_pairs={{224,0},{192,32},{160,64},{128,96},{96,128},{64,160},{32,192},{0,2... | collective-permute-start | bytes 1572872 | tf_op jit(solution)/shard_map/ppermute | solution.py:402
  36.9 1.2 copy-start.1
  40.9 31.8 %all-to-all-start.1 = ((f32[32,9,8,128]{3,2,1,0:T(8,128)}), f32[32,9,8,128]{3,2,1,0:T(8,128)S(1)}, u32[]{:S(2)}, u32[]{:S(2)}) async-start(f32[32,9,8,128]{3,2,1,0:T(8,128)} %x_forward.1), calls=%async_computation.1 | async-start | bytes 2359296 | tf_op jit(solution)/shard_map/all_to_all | solution.py:451
  53.9 1.0 copy-start.4
  54.9 0.9 copy-start.7
  55.8 1.6 %copy-start.9 = (f32[16,64,512]{2,1,0:T(8,128)S(1)}, f32[16,64,512]{2,1,0:T(8,128)}, u32[]{:S(2)}) copy-start(f32[16,64,512]{2,1,0:T(8,128)} %own.3) | copy-start | bytes 6291460
  70.1 7.6 %collective-permute-start.3 = (f32[1,32,512]{2,1,0:T(8,128)}, f32[1,32,512]{2,1,0:T(8,128)}, u32[]{:S(2)}, u32[]{:S(2)}) collective-permute-start(f32[1,32,512]{2,1,0:T(8,128)} %slice.4), channel_id=1, source_target_pairs={{0,1},{1,2},{2,3},{3,4},{4,5},{5,6},{6,7},{7,8},{8,9},{9,10},{10,1... | collective-permute-start | bytes 196616 | tf_op jit(solution)/shard_map/ppermute | solution.py:393
  72.6 1.2 copy-start.2
  73.9 3.8 %copy-start = (bf16[512,1024]{1,0:T(8,128)(2,1)S(1)}, bf16[512,1024]{1,0:T(8,128)(2,1)}, u32[]{:S(2)}) copy-start(bf16[512,1024]{1,0:T(8,128)(2,1)} %constant.12.clone.table.plain) | copy-start | bytes 3145732
  81.5 23.7 %copy-start.3 = (bf16[512,1024]{1,0:T(8,128)(2,1)S(1)}, bf16[512,1024]{1,0:T(8,128)(2,1)}, u32[]{:S(2)}) copy-start(bf16[512,1024]{1,0:T(8,128)(2,1)} %constant.13.clone.table) | copy-start | bytes 3145732
  105.1 26.9 %copy-start.6 = (bf16[1920,256]{1,0:T(8,128)(2,1)S(1)}, bf16[1920,256]{1,0:T(8,128)(2,1)}, u32[]{:S(2)}) copy-start(bf16[1920,256]{1,0:T(8,128)(2,1)} %constant.14.clone.table) | copy-start | bytes 2949124
  106.9 25.2 %copy-start.5 = (f32[32,8,256]{2,1,0:T(8,128)S(1)}, f32[32,8,256]{2,1,0:T(8,128)}, u32[]{:S(2)}) copy-start(f32[32,8,256]{2,1,0:T(8,128)} %volume.5) | copy-start | bytes 786436
  106.9 25.2 %copy-start.8 = (f32[32,8,256]{2,1,0:T(8,128)S(1)}, f32[32,8,256]{2,1,0:T(8,128)}, u32[]{:S(2)}) copy-start(f32[32,8,256]{2,1,0:T(8,128)} %prior.3) | copy-start | bytes 786436
